TPU v7x, 256 devices: a whole 4x4x8 slice. The times are simulated.
256 devices in a mesh: dp: 8 (over z), zone: 32 (over x, y, core).
Axes of the slice: x: 4, y: 4, z: 8, core: 2. Of those that a mesh axis runs over, the one named last changes fastest.
Arguments:
- features: bfloat16 [8, 4096, 4096], P('dp', 'zone'), may hold values from -6 to 6
- query_states: bfloat16 [8, 4096, 4096], P('dp', 'zone'), may hold values from -160 to 160
- key_states: bfloat16 [8, 4096, 4096], P('dp', 'zone'), may hold values from -8 to 8
- value_states: bfloat16 [8, 4096, 4096], P('dp', 'zone'), may hold values from -6 to 6
- cotangent: bfloat16 [8, 4096, 4096], P('dp', 'zone'), may hold values from -144 to 144
- adapter_down: bfloat16 [2, 64, 4096], replicated, may hold values from -0.09375 to 0.09375
- adapter_up: bfloat16 [2, 64, 4096], replicated, may hold values from -0.09375 to 0.09375
- block_lists: int32 [8, 64, 8], P('dp', 'zone'), may hold values from 0 to 63, all different within a row
- block_counts: int32 [8, 64], P('dp', 'zone'), may hold values from 2 to 8
Outputs:
- query_grad: bfloat16 [8, 4096, 4096], P('dp', 'zone')
- key_grad: bfloat16 [8, 4096, 4096], P('dp', 'zone')
- value_grad: bfloat16 [8, 4096, 4096], P('dp', 'zone')
- down_grad: float32 [2, 64, 4096], P(None, None, 'zone')
- up_grad: float32 [2, 64, 4096], P(None, None, 'zone')
Inputs may be any that keep to these rules, and one draw needn't show every extreme that they name: `block_lists`: each block's 8 entries are different blocks of its window, possibly itself; only the first block_counts entries are read.
All inputs are finite; a program needn't handle non-finite values.
Results may differ from a plain program's by a relative error of at most 0.0074.
Values may be sent and summed in bfloat16 or wider, within the bound.
No kernel may reach another device: no remote copies, remote signals or barrier semaphores. Data moves between devices by JAX's collectives and lax.ppermute only.
A program may use at most 64 MiB of HBM per device.

v0:
```python
import math

import jax
import jax.numpy as jnp
from jax import lax
from jax.sharding import PartitionSpec as P

HEAD = 128
BLK = 64


def shards(
    features,
    query_states,
    key_states,
    value_states,
    cotangent,
    adapter_down,
    adapter_up,
    block_lists,
    block_counts,
):
    zone_count = lax.axis_size("zone")
    row_count = query_states.shape[1]
    feature_count = query_states.shape[2]
    head_span = feature_count // zone_count
    heads_here = head_span // HEAD
    scale = HEAD ** (-0.5)

    def spread(states):
        return states[0].reshape(row_count, zone_count, head_span)

    moved = (
        lax.all_to_all(spread(query_states), "zone", split_axis=1, concat_axis=0, tiled=True),
        lax.all_to_all(spread(key_states), "zone", split_axis=1, concat_axis=0, tiled=True),
        lax.all_to_all(spread(value_states), "zone", split_axis=1, concat_axis=0, tiled=True),
        lax.all_to_all(spread(cotangent), "zone", split_axis=1, concat_axis=0, tiled=True),
    )
    all_rows = zone_count * row_count
    block_total = all_rows // BLK

    def blocked(states):
        return states.reshape(block_total, BLK, heads_here, HEAD)

    query_all = blocked(moved[0])
    key_all = blocked(moved[1])
    value_all = blocked(moved[2])
    grad_all = blocked(moved[3])
    lists, counts = (
        lax.all_gather(block_lists, "zone", axis=1, tiled=True),
        lax.all_gather(block_counts, "zone", axis=1, tiled=True),
    )
    own_ids = jnp.arange(block_total, dtype=jnp.int32)[:, None]
    slot_ids = jnp.concatenate([own_ids, lists[0]], axis=1)
    slot_count = slot_ids.shape[1]
    slot_valid = jnp.arange(slot_count, dtype=jnp.int32)[None, :] < counts[0][:, None] + 1
    group = math.gcd(block_total, 8)
    rounds = block_total // group

    def one_round(carried, position):
        key_acc, value_acc = carried
        first = position * group
        ids_here = lax.dynamic_slice_in_dim(slot_ids, first, group, 0)
        used = lax.dynamic_slice_in_dim(slot_valid, first, group, 0)
        query_grp = lax.dynamic_slice_in_dim(query_all, first, group, 0)
        grad_grp = lax.dynamic_slice_in_dim(grad_all, first, group, 0)
        key_grp = key_all[ids_here]
        value_grp = value_all[ids_here]
        scores = (
            jnp.einsum("gipd,gskpd->gpisk", query_grp, key_grp, preferred_element_type=jnp.float32)
            * scale
        )
        scores = jnp.where(used[:, None, None, :, None], scores, -jnp.inf)
        highest = jnp.max(scores, axis=(3, 4), keepdims=True)
        expd = jnp.exp(scores - highest)
        weights = expd / jnp.sum(expd, axis=(3, 4), keepdims=True)
        weights_b = weights.astype(jnp.bfloat16)
        attended = jnp.einsum(
            "gpisk,gskpd->gipd", weights_b, value_grp, preferred_element_type=jnp.float32
        )
        delta = jnp.sum(grad_grp.astype(jnp.float32) * attended, axis=-1)
        grad_weights = jnp.einsum(
            "gipd,gskpd->gpisk", grad_grp, value_grp, preferred_element_type=jnp.float32
        )
        grad_scores = (
            weights * (grad_weights - delta.transpose(0, 2, 1)[:, :, :, None, None])
        ).astype(jnp.bfloat16)
        query_part = (
            jnp.einsum(
                "gpisk,gskpd->gipd", grad_scores, key_grp, preferred_element_type=jnp.float32
            )
            * scale
        ).astype(jnp.bfloat16)
        key_part = (
            jnp.einsum(
                "gpisk,gipd->gskpd", grad_scores, query_grp, preferred_element_type=jnp.float32
            )
            * scale
        )
        value_part = jnp.einsum(
            "gpisk,gipd->gskpd", weights_b, grad_grp, preferred_element_type=jnp.float32
        )
        flat_ids = ids_here.reshape(-1)
        key_acc = key_acc.at[flat_ids].add(
            key_part.reshape(group * slot_count, BLK, heads_here, HEAD)
        )
        value_acc = value_acc.at[flat_ids].add(
            value_part.reshape(group * slot_count, BLK, heads_here, HEAD)
        )
        return ((key_acc, value_acc), query_part)

    empty = jnp.zeros((block_total, BLK, heads_here, HEAD), jnp.float32)
    (key_acc, value_acc), query_blocks = lax.scan(one_round, (empty, empty), jnp.arange(rounds))

    def home(states):
        return states.reshape(zone_count, row_count, head_span)

    returned = (
        lax.all_to_all(home(query_blocks), "zone", split_axis=0, concat_axis=2, tiled=True),
        lax.all_to_all(
            home(key_acc.astype(jnp.bfloat16)), "zone", split_axis=0, concat_axis=2, tiled=True
        ),
        lax.all_to_all(
            home(value_acc.astype(jnp.bfloat16)), "zone", split_axis=0, concat_axis=2, tiled=True
        ),
    )
    query_grad, key_grad, value_grad = returned
    rows_x = features[0]
    stacked = jnp.stack([key_grad[0], value_grad[0]])
    lowrank = jnp.einsum(
        "rd,tad->tra", rows_x, adapter_down, preferred_element_type=jnp.float32
    ).astype(jnp.bfloat16)
    up_term = jnp.einsum("tra,trh->tah", lowrank, stacked, preferred_element_type=jnp.float32)
    back_low = jnp.einsum(
        "trh,tah->tra", stacked, adapter_up, preferred_element_type=jnp.float32
    ).astype(jnp.bfloat16)
    down_term = jnp.einsum("tra,rd->tad", back_low, rows_x, preferred_element_type=jnp.float32)
    factor = 1.0 / math.sqrt(lax.axis_size("dp") * all_rows)
    summed = lax.psum((down_term, up_term), "dp")
    shares = (
        lax.psum_scatter(summed[0], "zone", scatter_dimension=2, tiled=True),
        lax.psum_scatter(summed[1], "zone", scatter_dimension=2, tiled=True),
    )
    down_share = shares[0]
    up_share = shares[1]
    return (query_grad, key_grad, value_grad, down_share * factor, up_share * factor)


def solution(mesh):
    in_specs = (
        P("dp", "zone", None),
        P("dp", "zone", None),
        P("dp", "zone", None),
        P("dp", "zone", None),
        P("dp", "zone", None),
        P(),
        P(),
        P("dp", "zone", None),
        P("dp", "zone"),
    )
    out_specs = (
        P("dp", "zone", None),
        P("dp", "zone", None),
        P("dp", "zone", None),
        P(None, None, "zone"),
        P(None, None, "zone"),
    )
    return jax.shard_map(shards, mesh=mesh, in_specs=in_specs, out_specs=out_specs, check_vma=False)
```

profile of v0, /device:TPU:2, one launch (start us, length us, event | category | flops | bytes accessed | tf_op | source)
XLA Modules:
  0.0 799.1 jit_solution(12996964444711800413)
XLA Ops:
  10.1 7.6 all-to-all-start
  19.1 13.1 %all-to-all-done = bf16[128,32,128]{2,0,1:T(8,128)(2,1)S(1)} async-done(((bf16[128,32,128]{2,0,1:T(8,128)(2,1)}), bf16[128,32,128]{2,0,1:T(8,128)(2,1)S(1)}, u32[]{:S(2)}, u32[]{:S(2)}) %all-to-all-start) | async-done | bytes 1048608 | tf_op jit(solution)/shard_map/all_to_all | solution.py:34
  32.2 6.4 all-to-all-start.1
  40.9 12.2 %all-to-all-done.1 = bf16[128,32,128]{0,2,1:T(8,128)(2,1)S(1)} async-done(((bf16[128,32,128]{0,2,1:T(8,128)(2,1)}), bf16[128,32,128]{0,2,1:T(8,128)(2,1)S(1)}, u32[]{:S(2)}, u32[]{:S(2)}) %all-to-all-start.1) | async-done | bytes 1048608 | tf_op jit(solution)/shard_map/all_to_all | solution.py:35
  53.1 6.4 all-to-all-start.3
  62.4 11.6 %all-to-all-done.3 = bf16[128,32,128]{0,2,1:T(8,128)(2,1)S(1)} async-done(((bf16[128,32,128]{0,2,1:T(8,128)(2,1)}), bf16[128,32,128]{0,2,1:T(8,128)(2,1)S(1)}, u32[]{:S(2)}, u32[]{:S(2)}) %all-to-all-start.3) | async-done | bytes 1048608 | tf_op jit(solution)/shard_map/all_to_all | solution.py:36
  74.9 6.4 all-to-all-start.2
  81.4 30.5 %all_gather.6 = s32[1,64,8]{2,0,1:T(1,128)S(1)} all-gather(s32[1,2,8]{2,0,1:T(1,128)S(1)} %bitcast.237), channel_id=1, replica_groups=mesh['dp'=8,'zone'=32] {'zone'}, dimensions={1}, use_global_device_ids=true | all-gather | bytes 2112 | tf_op jit(solution)/shard_map/all_gather | solution.py:50
  113.4 14.2 %all-reduce = s32[64]{0:T(128)S(1)} all-reduce(s32[64]{0:T(128)S(1)} %bitcast_dynamic-update-slice_fusion), channel_id=1, replica_groups=mesh['dp'=8,'zone'=32] {'zone'}, use_global_device_ids=true, to_apply=%add | all-reduce | flops 64 | bytes 512
  134.2 355.9 %while.14 = (s32[]{:T(128)}, f32[64,64,1,128]{3,1,0,2:T(8,128)S(1)}, f32[64,64,1,128]{3,1,0,2:T(8,128)}, bf16[8,8,64,1,128]{4,2,1,3,0:T(8,128)(2,1)}, s32[8]{0:T...) while((s32[]{:T(128)}, ...), condition=%wide.region_6.7_spmd, body=%wide.region_0.6_spmd.sunk | while | flops 460685248 | bytes 67791568 | solution.py:113
  150.7 12.6 %scatter_fusion = f32[64,64,128]{2,1,0:T(8,128)} fusion(f32[64,64,128]{2,1,0:T(8,128)} %bitcast.215, s32[72]{0:T(128)S(1)} %fusion.75, f32[72,64,128]{2,1,0:T(8,128)} %bitcast.212), kind=kCustom, calls=%fused_computation.2.clone.1 | custom fusion | flops 589824 | bytes 7078176 | tf_op jit(solution)/shard_map/while/body/eval_jaxpr/scatter-add | solution.py:104
  166.1 12.7 %scatter_fusion.1 = f32[64,64,128]{2,1,0:T(8,128)} fusion(f32[64,64,128]{2,1,0:T(8,128)} %bitcast.205, s32[72]{0:T(128)S(1)} %fusion.75, f32[72,64,128]{2,1,0:T(8,128)} %bitcast.213), kind=kCustom, calls=%fused_computation.3.clone.1 | custom fusion | flops 589824 | bytes 7078176 | tf_op jit(solution)/shard_map/while/body/eval_jaxpr/scatter-add | solution.py:107
  195.2 12.6 %scatter_fusion = f32[64,64,128]{2,1,0:T(8,128)} fusion(f32[64,64,128]{2,1,0:T(8,128)} %bitcast.215, s32[72]{0:T(128)S(1)} %fusion.75, f32[72,64,128]{2,1,0:T(8,128)} %bitcast.212), kind=kCustom, calls=%fused_computation.2.clone.1 | custom fusion | flops 589824 | bytes 7078176 | tf_op jit(solution)/shard_map/while/body/eval_jaxpr/scatter-add | solution.py:104
  210.6 12.6 %scatter_fusion.1 = f32[64,64,128]{2,1,0:T(8,128)} fusion(f32[64,64,128]{2,1,0:T(8,128)} %bitcast.205, s32[72]{0:T(128)S(1)} %fusion.75, f32[72,64,128]{2,1,0:T(8,128)} %bitcast.213), kind=kCustom, calls=%fused_computation.3.clone.1 | custom fusion | flops 589824 | bytes 7078176 | tf_op jit(solution)/shard_map/while/body/eval_jaxpr/scatter-add | solution.py:107
  239.7 12.6 %scatter_fusion = f32[64,64,128]{2,1,0:T(8,128)} fusion(f32[64,64,128]{2,1,0:T(8,128)} %bitcast.215, s32[72]{0:T(128)S(1)} %fusion.75, f32[72,64,128]{2,1,0:T(8,128)} %bitcast.212), kind=kCustom, calls=%fused_computation.2.clone.1 | custom fusion | flops 589824 | bytes 7078176 | tf_op jit(solution)/shard_map/while/body/eval_jaxpr/scatter-add | solution.py:104
  255.1 12.7 %scatter_fusion.1 = f32[64,64,128]{2,1,0:T(8,128)} fusion(f32[64,64,128]{2,1,0:T(8,128)} %bitcast.205, s32[72]{0:T(128)S(1)} %fusion.75, f32[72,64,128]{2,1,0:T(8,128)} %bitcast.213), kind=kCustom, calls=%fused_computation.3.clone.1 | custom fusion | flops 589824 | bytes 7078176 | tf_op jit(solution)/shard_map/while/body/eval_jaxpr/scatter-add | solution.py:107
  284.2 12.6 %scatter_fusion = f32[64,64,128]{2,1,0:T(8,128)} fusion(f32[64,64,128]{2,1,0:T(8,128)} %bitcast.215, s32[72]{0:T(128)S(1)} %fusion.75, f32[72,64,128]{2,1,0:T(8,128)} %bitcast.212), kind=kCustom, calls=%fused_computation.2.clone.1 | custom fusion | flops 589824 | bytes 7078176 | tf_op jit(solution)/shard_map/while/body/eval_jaxpr/scatter-add | solution.py:104
  299.6 12.7 %scatter_fusion.1 = f32[64,64,128]{2,1,0:T(8,128)} fusion(f32[64,64,128]{2,1,0:T(8,128)} %bitcast.205, s32[72]{0:T(128)S(1)} %fusion.75, f32[72,64,128]{2,1,0:T(8,128)} %bitcast.213), kind=kCustom, calls=%fused_computation.3.clone.1 | custom fusion | flops 589824 | bytes 7078176 | tf_op jit(solution)/shard_map/while/body/eval_jaxpr/scatter-add | solution.py:107
  328.7 12.6 %scatter_fusion = f32[64,64,128]{2,1,0:T(8,128)} fusion(f32[64,64,128]{2,1,0:T(8,128)} %bitcast.215, s32[72]{0:T(128)S(1)} %fusion.75, f32[72,64,128]{2,1,0:T(8,128)} %bitcast.212), kind=kCustom, calls=%fused_computation.2.clone.1 | custom fusion | flops 589824 | bytes 7078176 | tf_op jit(solution)/shard_map/while/body/eval_jaxpr/scatter-add | solution.py:104
  344.1 12.6 %scatter_fusion.1 = f32[64,64,128]{2,1,0:T(8,128)} fusion(f32[64,64,128]{2,1,0:T(8,128)} %bitcast.205, s32[72]{0:T(128)S(1)} %fusion.75, f32[72,64,128]{2,1,0:T(8,128)} %bitcast.213), kind=kCustom, calls=%fused_computation.3.clone.1 | custom fusion | flops 589824 | bytes 7078176 | tf_op jit(solution)/shard_map/while/body/eval_jaxpr/scatter-add | solution.py:107
  373.1 12.6 %scatter_fusion = f32[64,64,128]{2,1,0:T(8,128)} fusion(f32[64,64,128]{2,1,0:T(8,128)} %bitcast.215, s32[72]{0:T(128)S(1)} %fusion.75, f32[72,64,128]{2,1,0:T(8,128)} %bitcast.212), kind=kCustom, calls=%fused_computation.2.clone.1 | custom fusion | flops 589824 | bytes 7078176 | tf_op jit(solution)/shard_map/while/body/eval_jaxpr/scatter-add | solution.py:104
  388.5 12.7 %scatter_fusion.1 = f32[64,64,128]{2,1,0:T(8,128)} fusion(f32[64,64,128]{2,1,0:T(8,128)} %bitcast.205, s32[72]{0:T(128)S(1)} %fusion.75, f32[72,64,128]{2,1,0:T(8,128)} %bitcast.213), kind=kCustom, calls=%fused_computation.3.clone.1 | custom fusion | flops 589824 | bytes 7078176 | tf_op jit(solution)/shard_map/while/body/eval_jaxpr/scatter-add | solution.py:107
  417.6 12.6 %scatter_fusion = f32[64,64,128]{2,1,0:T(8,128)} fusion(f32[64,64,128]{2,1,0:T(8,128)} %bitcast.215, s32[72]{0:T(128)S(1)} %fusion.75, f32[72,64,128]{2,1,0:T(8,128)} %bitcast.212), kind=kCustom, calls=%fused_computation.2.clone.1 | custom fusion | flops 589824 | bytes 7078176 | tf_op jit(solution)/shard_map/while/body/eval_jaxpr/scatter-add | solution.py:104
  433.0 12.7 %scatter_fusion.1 = f32[64,64,128]{2,1,0:T(8,128)} fusion(f32[64,64,128]{2,1,0:T(8,128)} %bitcast.205, s32[72]{0:T(128)S(1)} %fusion.75, f32[72,64,128]{2,1,0:T(8,128)} %bitcast.213), kind=kCustom, calls=%fused_computation.3.clone.1 | custom fusion | flops 589824 | bytes 7078176 | tf_op jit(solution)/shard_map/while/body/eval_jaxpr/scatter-add | solution.py:107
  462.1 12.6 %scatter_fusion = f32[64,64,128]{2,1,0:T(8,128)} fusion(f32[64,64,128]{2,1,0:T(8,128)} %bitcast.215, s32[72]{0:T(128)S(1)} %fusion.75, f32[72,64,128]{2,1,0:T(8,128)} %bitcast.212), kind=kCustom, calls=%fused_computation.2.clone.1 | custom fusion | flops 589824 | bytes 7078176 | tf_op jit(solution)/shard_map/while/body/eval_jaxpr/scatter-add | solution.py:104
  477.5 12.7 %scatter_fusion.1 = f32[64,64,128]{2,1,0:T(8,128)} fusion(f32[64,64,128]{2,1,0:T(8,128)} %bitcast.205, s32[72]{0:T(128)S(1)} %fusion.75, f32[72,64,128]{2,1,0:T(8,128)} %bitcast.213), kind=kCustom, calls=%fused_computation.3.clone.1 | custom fusion | flops 589824 | bytes 7078176 | tf_op jit(solution)/shard_map/while/body/eval_jaxpr/scatter-add | solution.py:107
  500.0 11.7 %all-to-all-done.5 = bf16[32,128,128]{2,1,0:T(8,128)(2,1)S(1)} async-done(((bf16[32,128,128]{2,1,0:T(8,128)(2,1)}), bf16[32,128,128]{2,1,0:T(8,128)(2,1)S(1)}, u32[]{:S(2)}, u32[]{:S(2)}) %all-to-all-start.5) | async-done | bytes 1048608 | tf_op jit(solution)/shard_map/all_to_all | solution.py:120
  511.6 6.9 all-to-all-start.6
  521.0 12.0 %all-to-all-done.6 = bf16[32,128,128]{2,1,0:T(8,128)(2,1)} async-done(((bf16[32,128,128]{2,1,0:T(8,128)(2,1)}), bf16[32,128,128]{2,1,0:T(8,128)(2,1)}, u32[]{:S(2)}, u32[]{:S(2)}) %all-to-all-start.6) | async-done | bytes 1048608 | tf_op jit(solution)/shard_map/all_to_all | solution.py:123
  549.8 77.5 %reduce-scatter.3.cloned.1.call-done = f32[2,64,128]{2,1,0:T(8,128)} async-done(((f32[2,64,4096]{2,1,0:T(8,128)}), f32[2,64,128]{2,1,0:T(8,128)}) %reduce-scatter.3.cloned.1.call-update) | async-done | bytes 65552 | tf_op jit(solution)/shard_map/reduce_scatter | solution.py:141
  627.2 89.7 %reduce-scatter.5.cloned.1.call-done = f32[2,64,128]{2,1,0:T(8,128)} async-done(((f32[2,64,4096]{2,1,0:T(8,128)}), f32[2,64,128]{2,1,0:T(8,128)}) %reduce-scatter.5.cloned.1.call-update) | async-done | bytes 65552 | tf_op jit(solution)/shard_map/reduce_scatter | solution.py:142
  719.0 72.1 %all-reduce.4.cloned.1.call-done = (f32[2,64,128]{2,1,0:T(8,128)}, f32[2,64,128]{2,1,0:T(8,128)}) async-done(((f32[2,64,128]{2,1,0:T(8,128)}, f32[2,64,128]{2,1,0:T(8,128)}), (f32[2,64,128]{2,1,0:T(8,128)}, f32[2,64,128]{2,1,0:T(8,128)})) %all-reduce.4.cloned.1.call-update) | async-done | bytes 131088 | tf_op jit(solution)/shard_map/psum | solution.py:139
  (266 shorter events, 198.1 us)
Async XLA Ops:
  7.2 528.4 %copy-start = (bf16[1,128,4096]{2,1,0:T(8,128)(2,1)S(1)}, bf16[1,128,4096]{2,1,0:T(8,128)(2,1)}, u32[]{:S(2)}) copy-start(bf16[1,128,4096]{2,1,0:T(8,128)(2,1)} %param.11) | copy-start | bytes 3145732
  8.7 9.0 %copy-start.9 = (bf16[1,128,4096]{2,1,0:T(8,128)(2,1)S(1)}, bf16[1,128,4096]{2,1,0:T(8,128)(2,1)}, u32[]{:S(2)}) copy-start(bf16[1,128,4096]{2,1,0:T(8,128)(2,1)} %param.13) | copy-start | bytes 3145732
  10.1 22.1 %all-to-all-start = ((bf16[128,32,128]{2,0,1:T(8,128)(2,1)}), bf16[128,32,128]{2,0,1:T(8,128)(2,1)S(1)}, u32[]{:S(2)}, u32[]{:S(2)}) async-start(bf16[128,32,128]{2,0,1:T(8,128)(2,1)} %copy.63), calls=%async_computation | async-start | bytes 2097152 | tf_op jit(solution)/shard_map/all_to_all | solution.py:34
  32.2 8.7 %copy-start.5 = (bf16[128,32,128]{2,0,1:T(8,128)(2,1)}, bf16[128,32,128]{2,0,1:T(8,128)(2,1)S(1)}, u32[]{:S(2)}) copy-start(bf16[128,32,128]{2,0,1:T(8,128)(2,1)S(1)} %all-to-all-done) | copy-start | bytes 3145732
  32.2 20.9 %all-to-all-start.1 = ((bf16[128,32,128]{0,2,1:T(8,128)(2,1)}), bf16[128,32,128]{0,2,1:T(8,128)(2,1)S(1)}, u32[]{:S(2)}, u32[]{:S(2)}) async-start(bf16[128,32,128]{0,2,1:T(8,128)(2,1)} %bitcast.230), calls=%async_computation.1 | async-start | bytes 2097152 | tf_op jit(solution)/shard_map/all_to_all | solution.py:35
  53.1 20.9 %all-to-all-start.3 = ((bf16[128,32,128]{0,2,1:T(8,128)(2,1)}), bf16[128,32,128]{0,2,1:T(8,128)(2,1)S(1)}, u32[]{:S(2)}, u32[]{:S(2)}) async-start(bf16[128,32,128]{0,2,1:T(8,128)(2,1)} %bitcast.229), calls=%async_computation.3 | async-start | bytes 2097152 | tf_op jit(solution)/shard_map/all_to_all | solution.py:36
  60.9 20.4 %copy-start.10 = (s32[1,2,8]{2,1,0:T(2,128)S(1)}, s32[1,2,8]{2,1,0:T(2,128)}, u32[]{:S(2)}) copy-start(s32[1,2,8]{2,1,0:T(2,128)} %param.18) | copy-start | bytes 196
  61.0 51.1 %copy-start.12 = (u32[256]{0:T(256)S(1)}, u32[256]{0:T(256)}, u32[]{:S(2)}) copy-start(u32[256]{0:T(256)} %constant.44) | copy-start | bytes 3076
  61.0 52.3 %copy-start.11 = (s32[1,2]{1,0:T(1,128)S(1)}, s32[1,2]{1,0:T(1,128)}, u32[]{:S(2)}) copy-start(s32[1,2]{1,0:T(1,128)} %param.19) | copy-start | bytes 28
  74.9 56.3 %all-to-all-start.2 = ((bf16[128,32,128]{2,0,1:T(8,128)(2,1)}), bf16[128,32,128]{2,0,1:T(8,128)(2,1)S(1)}, u32[]{:S(2)}, u32[]{:S(2)}) async-start(bf16[128,32,128]{2,0,1:T(8,128)(2,1)} %copy.66), calls=%async_computation.2 | async-start | bytes 2097152 | tf_op jit(solution)/shard_map/all_to_all | solution.py:37
  135.8 2.1 copy-start.4
  166.1 12.7 %copy-start.2 = (f32[64,64,128]{2,1,0:T(8,128)S(1)}, f32[64,64,128]{2,1,0:T(8,128)}, u32[]{:S(2)}) copy-start(f32[64,64,128]{2,1,0:T(8,128)} %scatter_fusion) | copy-start | bytes 6291460 | tf_op jit(solution)/shard_map/while
  180.3 2.1 copy-start.4
  210.6 12.6 %copy-start.2 = (f32[64,64,128]{2,1,0:T(8,128)S(1)}, f32[64,64,128]{2,1,0:T(8,128)}, u32[]{:S(2)}) copy-start(f32[64,64,128]{2,1,0:T(8,128)} %scatter_fusion) | copy-start | bytes 6291460 | tf_op jit(solution)/shard_map/while
  224.8 2.1 copy-start.4
  255.1 12.7 %copy-start.2 = (f32[64,64,128]{2,1,0:T(8,128)S(1)}, f32[64,64,128]{2,1,0:T(8,128)}, u32[]{:S(2)}) copy-start(f32[64,64,128]{2,1,0:T(8,128)} %scatter_fusion) | copy-start | bytes 6291460 | tf_op jit(solution)/shard_map/while
  269.3 2.1 copy-start.4
  299.6 12.7 %copy-start.2 = (f32[64,64,128]{2,1,0:T(8,128)S(1)}, f32[64,64,128]{2,1,0:T(8,128)}, u32[]{:S(2)}) copy-start(f32[64,64,128]{2,1,0:T(8,128)} %scatter_fusion) | copy-start | bytes 6291460 | tf_op jit(solution)/shard_map/while
  313.8 2.1 copy-start.4
  344.1 12.6 %copy-start.2 = (f32[64,64,128]{2,1,0:T(8,128)S(1)}, f32[64,64,128]{2,1,0:T(8,128)}, u32[]{:S(2)}) copy-start(f32[64,64,128]{2,1,0:T(8,128)} %scatter_fusion) | copy-start | bytes 6291460 | tf_op jit(solution)/shard_map/while
  388.5 12.7 %copy-start.2 = (f32[64,64,128]{2,1,0:T(8,128)S(1)}, f32[64,64,128]{2,1,0:T(8,128)}, u32[]{:S(2)}) copy-start(f32[64,64,128]{2,1,0:T(8,128)} %scatter_fusion) | copy-start | bytes 6291460 | tf_op jit(solution)/shard_map/while
  402.7 2.1 copy-start.4
  433.0 12.7 %copy-start.2 = (f32[64,64,128]{2,1,0:T(8,128)S(1)}, f32[64,64,128]{2,1,0:T(8,128)}, u32[]{:S(2)}) copy-start(f32[64,64,128]{2,1,0:T(8,128)} %scatter_fusion) | copy-start | bytes 6291460 | tf_op jit(solution)/shard_map/while
  447.2 2.1 copy-start.4
  477.5 12.7 %copy-start.2 = (f32[64,64,128]{2,1,0:T(8,128)S(1)}, f32[64,64,128]{2,1,0:T(8,128)}, u32[]{:S(2)}) copy-start(f32[64,64,128]{2,1,0:T(8,128)} %scatter_fusion) | copy-start | bytes 6291460 | tf_op jit(solution)/shard_map/while
  491.3 20.3 %all-to-all-start.5 = ((bf16[32,128,128]{2,1,0:T(8,128)(2,1)}), bf16[32,128,128]{2,1,0:T(8,128)(2,1)S(1)}, u32[]{:S(2)}, u32[]{:S(2)}) async-start(bf16[32,128,128]{2,1,0:T(8,128)(2,1)} %bitcast.226), calls=%async_computation.5 | async-start | bytes 2097152 | tf_op jit(solution)/shard_map/all_to_all | solution.py:120
  511.6 6.9 copy-start.7
  511.6 21.5 %all-to-all-start.6 = ((bf16[32,128,128]{2,1,0:T(8,128)(2,1)}), bf16[32,128,128]{2,1,0:T(8,128)(2,1)}, u32[]{:S(2)}, u32[]{:S(2)}) async-start(bf16[32,128,128]{2,1,0:T(8,128)(2,1)} %bitcast.60), calls=%async_computation.6 | async-start | bytes 2097152 | tf_op jit(solution)/shard_map/all_to_all | solution.py:123
  518.5 108.7 %reduce-scatter.3.cloned.1.call-start = ((), (), s32[]{:S(2)}) async-start(), calls=%async_computation.9 | async-start | bytes 2162688 | tf_op jit(solution)/shard_map/reduce_scatter | solution.py:141
  539.4 177.6 %reduce-scatter.5.cloned.1.call-start = ((), (), s32[]{:S(2)}) async-start(), calls=%async_computation.10 | async-start | bytes 2162688 | tf_op jit(solution)/shard_map/reduce_scatter | solution.py:142
  543.3 173.7 %all-to-all-start.4 = ((bf16[32,128,128]{2,1,0:T(8,128)(2,1)}), bf16[32,128,128]{2,1,0:T(8,128)(2,1)S(1)}, u32[]{:S(2)}, u32[]{:S(2)}) async-start(bf16[32,128,128]{2,1,0:T(8,128)(2,1)} %bitcast.53), calls=%async_computation.4 | async-start | bytes 2097152 | tf_op jit(solution)/shard_map/all_to_all | solution.py:119
  549.7 241.4 %all-reduce.4.cloned.1.call-start = ((), (), s32[]{:S(2)}) async-start(), calls=%async_computation.11 | async-start | bytes 262144 | tf_op jit(solution)/shard_map/psum | solution.py:139
  (19 other events, 26.9 us)
Sparse Core Ops, SparseCore 0:
  539.5 87.7 reduce-scatter.2
  631.1 85.8 reduce-scatter.4
  719.3 71.7 all-reduce.3
where the time goes:
time: 804 us; the launch traced here: 799 us
  waiting for transfers between devices  300 us (37%)
  other arithmetic  232 us (29%)
  matrix products  88.2 us (11%)
  local copies, waits for them, and re-layouts  67.8 us (8%)
  starting transfers between devices  46.2 us (6%)
  blocking collectives  44.7 us (6%)
  between operations  14.6 us (2%)
    scatter-add x8, other arithmetic, one_round(): value_acc.at[flat_ids]  101 us
    scatter-add x8, other arithmetic, one_round(): key_acc.at[flat_ids]  101 us
    reduce_scatter x1, waiting for transfers between devices, shards(): lax.psum_scatter(summed[1], 'zone', scatter_dimension=2, tiled=True)  89.7 us
    reduce_scatter x1, waiting for transfers between devices, shards(): lax.psum_scatter(summed[0], 'zone', scatter_dimension=2, tiled=True)  77.5 us
    psum x1, waiting for transfers between devices, shards(): summed = lax.psum((down_term, up_term), 'dp')  72.1 us
    while x16, matrix products  33 us
    all_gather x1, blocking collectives, shards(): lax.all_gather(block_lists, 'zone', axis=1, tiled=True)  30.5 us
    gather x8, local copies, waits for them, and re-layouts, one_round(): key_grp = key_all[ids_here]  16.7 us
  transfers between devices with their start and end apart: 10, of which 8 were waited for; matrix products, arithmetic and copies ran while one was open for 3% of the time, Pallas kernels for 0%

commit v1 on v0

v1 whole, which is shorter than its diff:
```python
import functools
import math

import jax
import jax.numpy as jnp
from jax import lax
from jax.experimental import pallas as pl
from jax.experimental.pallas import tpu as pltpu
from jax.sharding import PartitionSpec as P

HEAD = 128
BLK = 64
VMEM_ALL = 60 << 20
META = 16
BF = jnp.bfloat16
F32 = jnp.float32
NT = (((1,), (1,)), ((), ()))
TN = (((0,), (0,)), ((), ()))
NN = (((1,), (0,)), ((), ()))


def dot(a, b, dims):
    return lax.dot_general(a, b, dims, preferred_element_type=F32)


def whole(shape, space=pltpu.VMEM):
    return pl.BlockSpec(memory_space=space)


def pack_kernel(meta_ref, q_ref, k_ref, v_ref, g_ref, out_ref):
    rows = q_ref.shape[0]
    for j in range(out_ref.shape[0]):
        cols = slice(j * HEAD, (j + 1) * HEAD)
        for t, ref in enumerate((q_ref, k_ref, v_ref, g_ref)):
            out_ref[j, t * rows:(t + 1) * rows, :] = ref[:, cols]
        out_ref[j, 4 * rows:, :] = meta_ref[...]


def pack(meta, q, k, v, g, heads_per_step=8):
    rows, feats = q.shape
    heads = feats // HEAD
    out_rows = 4 * rows + META
    spec = pl.BlockSpec((rows, heads_per_step * HEAD), lambda i: (0, i))
    return pl.pallas_call(
        pack_kernel,
        grid=(heads // heads_per_step,),
        in_specs=[pl.BlockSpec((META, HEAD), lambda i: (0, 0))] + [spec] * 4,
        out_specs=pl.BlockSpec((heads_per_step, out_rows, HEAD), lambda i: (i, 0, 0)),
        out_shape=jax.ShapeDtypeStruct((heads, out_rows, HEAD), BF),
        compiler_params=pltpu.CompilerParams(vmem_limit_bytes=VMEM_ALL),
        cost_estimate=pl.CostEstimate(flops=0, bytes_accessed=16 * rows * feats, transcendentals=0),
        name="pack",
    )(meta, q, k, v, g)


def attention_kernel(ids_ref, counts_ref, states_ref, out_ref, dk_ref, dv_ref, *, rows, slots):
    pairs = out_ref.shape[0]
    stride = 4 * rows + META
    scale = HEAD ** (-0.5)
    dk_ref[...] = jnp.zeros_like(dk_ref)
    dv_ref[...] = jnp.zeros_like(dv_ref)
    first_half = lax.broadcasted_iota(jnp.int32, (1, 2 * BLK), 1) < BLK

    def body(p, carry):
        base = p * stride

        def load(row, n):
            return states_ref[pl.ds(pl.multiple_of(row, 16), n), :]

        def blockdiag(x):
            zero = jnp.zeros((BLK, HEAD), BF)
            return jnp.concatenate(
                [
                    jnp.concatenate([x[:BLK], zero], axis=1),
                    jnp.concatenate([zero, x[BLK:]], axis=1),
                ],
                axis=0,
            )

        q_bd = blockdiag(load(base, rows))
        g_bd = blockdiag(load(base + 3 * rows, rows))
        ids = []
        k_parts = []
        v_parts = []
        for s in range(slots):
            pair_ids = [ids_ref[(2 * p + c) * slots + s] for c in range(2)]
            ids.append(pair_ids)
            at = [(i // 2) * stride + (i % 2) * BLK for i in pair_ids]
            k_parts.append(jnp.concatenate([load(a + rows, BLK) for a in at], axis=1))
            v_parts.append(jnp.concatenate([load(a + 2 * rows, BLK) for a in at], axis=1))
        k_cat = jnp.concatenate(k_parts, axis=0)
        v_cat = jnp.concatenate(v_parts, axis=0)
        count = jnp.where(first_half, counts_ref[2 * p], counts_ref[2 * p + 1])
        slot = lax.broadcasted_iota(jnp.int32, (slots * BLK, 2 * BLK), 0) // BLK
        scores = jnp.where(slot <= count, dot(k_cat, q_bd, NT), -jnp.inf)
        highest = jnp.max(scores, axis=0, keepdims=True)
        expd = jnp.exp((scores - highest) * scale)
        weights = expd * (1.0 / jnp.sum(expd, axis=0, keepdims=True))
        weights_b = weights.astype(BF)
        grad_weights = dot(v_cat, g_bd, NT)
        delta = jnp.sum(weights_b.astype(F32) * grad_weights, axis=0, keepdims=True)
        grad_scores = (weights * (grad_weights - delta)).astype(BF)
        dk = dot(grad_scores, q_bd, NN)
        dv = dot(weights_b, g_bd, NN)
        for s in range(slots):
            for c in range(2):
                at = pl.ds(pl.multiple_of(ids[s][c] * BLK, BLK), BLK)
                part = (slice(s * BLK, (s + 1) * BLK), slice(c * HEAD, (c + 1) * HEAD))
                dk_ref[at, :] += dk[part]
                dv_ref[at, :] += dv[part]
        dq = dot(grad_scores, k_cat, TN)
        out_ref[p, :BLK, :] = (dq[:BLK, :HEAD] * scale).astype(BF)
        out_ref[p, BLK:2 * BLK, :] = (dq[BLK:, HEAD:] * scale).astype(BF)
        return carry

    lax.fori_loop(0, pairs, body, 0)

    def finish(p, carry):
        at = pl.ds(pl.multiple_of(p * rows, rows), rows)
        out_ref[p, rows:2 * rows, :] = (dk_ref[at, :] * scale).astype(BF)
        out_ref[p, 2 * rows:, :] = dv_ref[at, :].astype(BF)
        return carry

    lax.fori_loop(0, pairs, finish, 0)


def attention(ids, counts, states, rows):
    pairs = states.shape[0]
    slots = ids.shape[1]
    all_rows = pairs * rows
    return pl.pallas_call(
        functools.partial(attention_kernel, rows=rows, slots=slots),
        in_specs=[
            pl.BlockSpec(memory_space=pltpu.SMEM),
            pl.BlockSpec(memory_space=pltpu.SMEM),
            pl.BlockSpec(memory_space=pltpu.VMEM),
        ],
        out_specs=pl.BlockSpec(memory_space=pltpu.VMEM),
        out_shape=jax.ShapeDtypeStruct((pairs, 3 * rows, HEAD), BF),
        scratch_shapes=[pltpu.VMEM((all_rows, HEAD), F32), pltpu.VMEM((all_rows, HEAD), F32)],
        compiler_params=pltpu.CompilerParams(vmem_limit_bytes=VMEM_ALL),
        cost_estimate=pl.CostEstimate(
            flops=2 * 5 * all_rows * slots * BLK * HEAD * 2,
            bytes_accessed=states.size * 2 + pairs * 3 * rows * HEAD * 2,
            transcendentals=all_rows * slots * BLK,
        ),
        name="attention",
    )(ids.reshape(-1), counts, states.reshape(-1, HEAD))


def down_kernel(grads_ref, up_ref, x_ref, out_ref):
    heads = grads_ref.shape[0]
    rows, feats = x_ref.shape
    low = []
    for t in range(2):
        total = jnp.zeros((rows, up_ref.shape[1]), F32)
        for h in range(heads):
            part = grads_ref[h, (1 + t) * rows:(2 + t) * rows, :]
            total += dot(part, up_ref[t, :, h * HEAD:(h + 1) * HEAD], NT)
        low.append(total)
    back_low = jnp.concatenate(low, axis=1).astype(BF)
    for h in range(heads):
        out_ref[h] = dot(back_low, x_ref[:, h * HEAD:(h + 1) * HEAD], TN).astype(BF)


def down_terms(grads, adapter_up, x):
    heads = grads.shape[0]
    rows, feats = x.shape
    return pl.pallas_call(
        down_kernel,
        in_specs=[pl.BlockSpec(memory_space=pltpu.VMEM)] * 3,
        out_specs=pl.BlockSpec(memory_space=pltpu.VMEM),
        out_shape=jax.ShapeDtypeStruct((heads, 2 * adapter_up.shape[1], HEAD), BF),
        compiler_params=pltpu.CompilerParams(vmem_limit_bytes=VMEM_ALL),
        cost_estimate=pl.CostEstimate(
            flops=8 * rows * feats * adapter_up.shape[1],
            bytes_accessed=12 * rows * feats,
            transcendentals=0,
        ),
        name="down_terms",
    )(grads, adapter_up, x)


def unpack_kernel(in_ref, q_ref, k_ref, v_ref):
    rows = q_ref.shape[0]
    for j in range(in_ref.shape[0]):
        cols = slice(j * HEAD, (j + 1) * HEAD)
        for t, ref in enumerate((q_ref, k_ref, v_ref)):
            ref[:, cols] = in_ref[j, t * rows:(t + 1) * rows, :]


def unpack(grads, heads_per_step=8):
    heads, rows3, _ = grads.shape
    rows = rows3 // 3
    shape = jax.ShapeDtypeStruct((rows, heads * HEAD), BF)
    spec = pl.BlockSpec((rows, heads_per_step * HEAD), lambda i: (0, i))
    return pl.pallas_call(
        unpack_kernel,
        grid=(heads // heads_per_step,),
        in_specs=[pl.BlockSpec((heads_per_step, rows3, HEAD), lambda i: (i, 0, 0))],
        out_specs=[spec] * 3,
        out_shape=[shape] * 3,
        compiler_params=pltpu.CompilerParams(vmem_limit_bytes=VMEM_ALL),
        cost_estimate=pl.CostEstimate(
            flops=0, bytes_accessed=12 * rows * heads * HEAD, transcendentals=0
        ),
        name="unpack",
    )(grads)


def swap(x, axis):
    return lax.all_to_all(x, axis, split_axis=0, concat_axis=0, tiled=True)


def shards(
    features,
    query_states,
    key_states,
    value_states,
    cotangent,
    adapter_down,
    adapter_up,
    block_lists,
    block_counts,
):
    zones = lax.axis_size("zone")
    windows = lax.axis_size("dp")
    rows = query_states.shape[1]
    rank = adapter_down.shape[1]
    all_rows = zones * rows
    blocks = all_rows // BLK
    own_blocks = rows // BLK
    nbr = block_lists.shape[2]
    x = features[0]

    meta = jnp.concatenate([block_lists[0], block_counts[0][:, None]], axis=1).astype(BF)
    meta = jnp.pad(meta, ((0, META - own_blocks), (0, HEAD - nbr - 1)))
    sent = pack(meta, query_states[0], key_states[0], value_states[0], cotangent[0])
    states = swap(sent, "zone")

    info = states[:, 4 * rows:4 * rows + own_blocks, :nbr + 1].astype(jnp.int32)
    info = info.reshape(blocks, nbr + 1)
    counts = info[:, nbr]
    own = jnp.arange(blocks, dtype=jnp.int32)[:, None]
    slot = jnp.arange(nbr, dtype=jnp.int32)[None, :]
    ids = jnp.concatenate([own, jnp.where(slot < counts[:, None], info[:, :nbr], own)], axis=1)

    low = dot(x, adapter_down.reshape(2 * rank, -1), NT).astype(BF)
    low = jnp.broadcast_to(low[None], (zones, rows, 2 * rank))
    low, states = lax.optimization_barrier((low, states))
    low_all = swap(low, "zone")

    grads = attention(ids, counts, states, rows)
    grads, low_all = lax.optimization_barrier((grads, low_all))
    home = swap(grads, "zone")

    stacked = grads.reshape(zones, 3, rows, HEAD)
    up = jnp.stack(
        [
            jnp.einsum(
                "zra,zrf->af",
                low_all[:, :, t * rank:(t + 1) * rank],
                stacked[:, 1 + t],
                preferred_element_type=F32,
            )
            for t in range(2)
        ]
    )
    up = lax.psum(up, "dp")

    terms = down_terms(home, adapter_up, x)
    terms = swap(terms, "zone")
    query_grad, key_grad, value_grad = unpack(home)
    down = jnp.sum(terms.astype(F32), axis=0)
    down = swap(jnp.broadcast_to(down.astype(BF)[None], (windows,) + down.shape), "dp")
    factor = 1.0 / math.sqrt(windows * all_rows)
    down = jnp.sum(down.astype(F32), axis=0).reshape(2, rank, HEAD) * factor
    return (query_grad[None], key_grad[None], value_grad[None], down, up * factor)


def solution(mesh):
    rows = P("dp", "zone", None)
    cols = P(None, None, "zone")
    in_specs = (rows, rows, rows, rows, rows, P(), P(), rows, P("dp", "zone"))
    out_specs = (rows, rows, rows, cols, cols)
    return jax.shard_map(shards, mesh=mesh, in_specs=in_specs, out_specs=out_specs, check_vma=False)
```

time: 804 us -> 288 us (0.36)
  other arithmetic: 232 us -> 5.08 us
  waiting for transfers between devices: 300 us -> 138 us
  matrix products: 88.2 us -> 3.56 us
  local copies, waits for them, and re-layouts: 67.8 us -> 4.07 us
  Pallas kernels: 0 us -> 47 us
  starting transfers between devices: 46.2 us -> 31.7 us
    scatter-add x16 -> x0, other arithmetic: 202 us -> none  [the longest x8 101 us: one_round(): value_acc.at[flat_ids]]
    reduce_scatter x2 -> x0, waiting for transfers between devices: 167 us -> none  [the longest x1 89.7 us: shards(): lax.psum_scatter(summed[1], 'zone', scatter_dimension=2, tiled=True)]
    dot_general x34 -> x3, matrix products: 55.2 us -> 3.56 us  [the longest x2 3.13 us: shards(): jnp.einsum('zra,zrf->af', low_all[:, :, t * rank:(t + 1) * rank], stacked...]
    pallas_call x0 -> x4, Pallas kernels: none -> 47 us  [the longest x1 32.8 us: attention(): pl.pallas_call(functools.partial(attention_kernel, rows=rows, slots=slots...]
    all_to_all x0 -> x1, blocking collectives: none -> 44.4 us  [swap(): return lax.all_to_all(x, axis, split_axis=0, concat_axis=0, tiled=True)]
    while x16 -> x0, matrix products: 33 us -> none
    gather x16 -> x0, local copies, waits for them, and re-layouts: 31.3 us -> none  [the longest x8 16.7 us: one_round(): key_grp = key_all[ids_here]]
    all_gather x1 -> x0, blocking collectives: 30.5 us -> none  [shards(): lax.all_gather(block_lists, 'zone', axis=1, tiled=True)]
  transfers between devices with their start and end apart: 10 -> 5, of which waited for: 8 -> 3; matrix products, arithmetic and copies ran while one was open for 3% -> 3% of each run, Pallas kernels for 0% -> 13%
where the time goes in v1:
time: 288 us; the launch traced here: 287 us
  waiting for transfers between devices  138 us (48%)
  Pallas kernels  47 us (16%)
  blocking collectives  44.4 us (15%)
  starting transfers between devices  31.7 us (11%)
  between operations  14.1 us (5%)
  other arithmetic  5.08 us (2%)
  local copies, waits for them, and re-layouts  4.07 us (1%)
  matrix products  3.56 us (1%)
    psum x1, waiting for transfers between devices, shards(): up = lax.psum(up, 'dp')  73.2 us
    all_to_all x4, waiting for transfers between devices, swap(): return lax.all_to_all(x, axis, split_axis=0, concat_axis=0, tiled=True)  64.3 us
    all_to_all x1, blocking collectives, swap(): return lax.all_to_all(x, axis, split_axis=0, concat_axis=0, tiled=True)  44.4 us
    pallas_call x1, Pallas kernels, attention(): pl.pallas_call(functools.partial(attention_kernel, rows=rows, slots=slots...  32.8 us
    all_to_all x4, starting transfers between devices, swap(): return lax.all_to_all(x, axis, split_axis=0, concat_axis=0, tiled=True)  31.7 us
  transfers between devices with their start and end apart: 5, of which 3 were waited for; matrix products, arithmetic and copies ran while one was open for 3% of the time, Pallas kernels for 13%

profile of v1, /device:TPU:2, one launch (start us, length us, event | category | flops | bytes accessed | tf_op | source)
XLA Modules:
  0.0 287.5 jit_solution(4465563646174426645)
XLA Ops:
  7.2 0.7 convert_bitcast_fusion
  7.9 0.1 copy.34
  8.0 0.7 convert_bitcast_fusion.1
  8.7 0.7 fusion.7.meta_ref
  9.4 5.0 %pack.1 = bf16[32,528,128]{2,1,0:T(8,128)(2,1)} custom-call(bf16[16,128]{1,0:T(8,128)(2,1)} %fusion.7.meta_ref, bf16[128,4096]{1,0:T(8,128)(2,1)} %bitcast.43, bf16[128,4096]{1,0:T(8,128)(2,1)} %bitcast.44, bf16[128,4096]{1,0:T(8,128)(2,1)} %bitcast.45, bf16[128,4096]{1,0:T(8,128)(2,1)} %bitcast.46), custom_call_target="tpu_custom_call" | custom-call | bytes 8388608 | tf_op jit(solution)/shard_map/pack/pallas_call | solution.py:44
  14.4 7.8 %all-to-all-start = ((bf16[32,528,128]{2,1,0:T(8,128)(2,1)}), bf16[32,528,128]{2,1,0:T(8,128)(2,1)}, u32[]{:S(2)}, u32[]{:S(2)}) async-start(bf16[32,528,128]{2,1,0:T(8,128)(2,1)} %pack.1), calls=%async_computation | async-start | bytes 8650752 | tf_op jit(solution)/shard_map/all_to_all | solution.py:212
  22.2 0.4 convolution_convert_fusion
  22.7 0.1 copy.38
  22.8 51.4 %all-to-all-done = bf16[32,528,128]{2,1,0:T(8,128)(2,1)} async-done(((bf16[32,528,128]{2,1,0:T(8,128)(2,1)}), bf16[32,528,128]{2,1,0:T(8,128)(2,1)}, u32[]{:S(2)}, u32[]{:S(2)}) %all-to-all-start) | async-done | bytes 4325408 | tf_op jit(solution)/shard_map/all_to_all | solution.py:212
  74.2 1.2 broadcast_in_dim.32
  75.4 9.0 %all-to-all-start.1 = ((bf16[32,128,128]{1,2,0:T(8,128)(2,1)}), bf16[32,128,128]{1,2,0:T(8,128)(2,1)S(1)}, u32[]{:S(2)}, u32[]{:S(2)}) async-start(bf16[32,128,128]{1,2,0:T(8,128)(2,1)} %broadcast_in_dim.32), calls=%async_computation.1 | async-start | bytes 2097152 | tf_op jit(solution)/shard_map/all_to_all | solution.py:212
  84.4 0.9 slice.28
  85.3 0.1 slice.29
  85.4 0.1 copy.41
  85.4 0.1 copy.42
  85.5 0.1 copy.37
  85.6 0.7 reshape.35.ids_ref
  86.4 32.8 %attention.1 = bf16[32,384,128]{2,1,0:T(8,128)(2,1)} custom-call(s32[576]{0:T(1024)} %reshape.35.ids_ref, s32[64]{0:T(128)} %bitcast.51, bf16[16896,128]{1,0:T(8,128)(2,1)} %bitcast.11.states_ref), custom_call_target="tpu_custom_call" | custom-call | flops 6039797760 | bytes 7471104 | tf_op jit(solution)/shard_map/attention/pallas_call | solution.py:131
  119.2 44.4 %all_to_all.25.in_ref.grads_ref = bf16[32,384,128]{2,1,0:T(8,128)(2,1)} all-to-all(bf16[32,384,128]{2,1,0:T(8,128)(2,1)} %attention.1), channel_id=1, replica_groups=mesh['dp'=8,'zone'=32] {'zone'}, dimensions={0} | all-to-all | bytes 6291456 | tf_op jit(solution)/shard_map/all_to_all | solution.py:212
  163.6 4.7 %down_terms.1 = bf16[32,128,128]{2,1,0:T(8,128)(2,1)} custom-call(bf16[32,384,128]{2,1,0:T(8,128)(2,1)} %all_to_all.25.in_ref.grads_ref, bf16[2,64,4096]{2,1,0:T(8,128)(2,1)} %up_ref.1, bf16[128,4096]{1,0:T(8,128)(2,1)} %bitcast.40), custom_call_target="tpu_custom_call" | custom-call | flops 268435456 | bytes 6291456 | tf_op jit(solution)/shard_map/down_terms/pallas_call | solution.py:169
  168.2 6.4 %all-to-all-start.3 = ((bf16[32,128,128]{2,1,0:T(8,128)(2,1)}), bf16[32,128,128]{2,1,0:T(8,128)(2,1)S(1)}, u32[]{:S(2)}, u32[]{:S(2)}) async-start(bf16[32,128,128]{2,1,0:T(8,128)(2,1)} %down_terms.1), calls=%async_computation.3 | async-start | bytes 2097152 | tf_op jit(solution)/shard_map/all_to_all | solution.py:212
  174.7 1.6 convolution_bitcast_fusion.1
  176.2 12.9 %all-to-all-done.3 = bf16[32,128,128]{2,1,0:T(8,128)(2,1)S(1)} async-done(((bf16[32,128,128]{2,1,0:T(8,128)(2,1)}), bf16[32,128,128]{2,1,0:T(8,128)(2,1)S(1)}, u32[]{:S(2)}, u32[]{:S(2)}) %all-to-all-start.3) | async-done | bytes 1048608 | tf_op jit(solution)/shard_map/all_to_all | solution.py:212
  189.1 0.2 reduce_sum.21
  189.3 0.7 broadcast_in_dim.36
  190.0 8.5 %all-to-all-start.4 = ((bf16[8,128,128]{2,1,0:T(8,128)(2,1)}), bf16[8,128,128]{2,1,0:T(8,128)(2,1)S(1)}, u32[]{:S(2)}, u32[]{:S(2)}) async-start(bf16[8,128,128]{2,1,0:T(8,128)(2,1)} %broadcast_in_dim.36), calls=%async_computation.4 | async-start | bytes 524288 | tf_op jit(solution)/shard_map/all_to_all | solution.py:212
  198.5 1.6 convolution_bitcast_fusion
  200.1 0.6 pad_maximum_fusion
  200.7 73.2 %all-reduce.3.cloned.1.call-done = f32[2,64,128]{2,1,0:T(8,128)} async-done(((f32[2,64,128]{2,1,0:T(8,128)}), f32[2,64,128]{2,1,0:T(8,128)}) %all-reduce.3.cloned.1.call-update) | async-done | bytes 65552 | tf_op jit(solution)/shard_map/psum | solution.py:269
  274.0 1.5 broadcast_multiply_fusion
  275.5 4.5 %unpack.1 = (bf16[128,4096]{1,0:T(8,128)(2,1)}, bf16[128,4096]{1,0:T(8,128)(2,1)}, bf16[128,4096]{1,0:T(8,128)(2,1)}) custom-call(bf16[32,384,128]{2,1,0:T(8,128)(2,1)} %all_to_all.25.in_ref.grads_ref), custom_call_target="tpu_custom_call" | custom-call | bytes 6291456 | tf_op jit(solution)/shard_map/unpack/pallas_call | solution.py:197
  280.0 0.6 broadcast_multiply_fusion.1
  (15 shorter events, 0.1 us)
Async XLA Ops:
  7.2 15.0 %copy-start = (bf16[2,64,4096]{2,1,0:T(8,128)(2,1)S(1)}, bf16[2,64,4096]{2,1,0:T(8,128)(2,1)}, u32[]{:S(2)}) copy-start(bf16[2,64,4096]{2,1,0:T(8,128)(2,1)} %param.14) | copy-start | bytes 3145732
  14.4 7.8 %copy-start.1 = (bf16[1,128,4096]{2,1,0:T(8,128)(2,1)S(1)}, bf16[1,128,4096]{2,1,0:T(8,128)(2,1)}, u32[]{:S(2)}) copy-start(bf16[1,128,4096]{2,1,0:T(8,128)(2,1)} %param.9) | copy-start | bytes 3145732
  14.4 59.8 %all-to-all-start = ((bf16[32,528,128]{2,1,0:T(8,128)(2,1)}), bf16[32,528,128]{2,1,0:T(8,128)(2,1)}, u32[]{:S(2)}, u32[]{:S(2)}) async-start(bf16[32,528,128]{2,1,0:T(8,128)(2,1)} %pack.1), calls=%async_computation | async-start | bytes 8650752 | tf_op jit(solution)/shard_map/all_to_all | solution.py:212
  75.4 43.7 %all-to-all-start.1 = ((bf16[32,128,128]{1,2,0:T(8,128)(2,1)}), bf16[32,128,128]{1,2,0:T(8,128)(2,1)S(1)}, u32[]{:S(2)}, u32[]{:S(2)}) async-start(bf16[32,128,128]{1,2,0:T(8,128)(2,1)} %broadcast_in_dim.32), calls=%async_computation.1 | async-start | bytes 2097152 | tf_op jit(solution)/shard_map/all_to_all | solution.py:212
  85.4 0.9 copy-start.2
  168.2 20.9 %all-to-all-start.3 = ((bf16[32,128,128]{2,1,0:T(8,128)(2,1)}), bf16[32,128,128]{2,1,0:T(8,128)(2,1)S(1)}, u32[]{:S(2)}, u32[]{:S(2)}) async-start(bf16[32,128,128]{2,1,0:T(8,128)(2,1)} %down_terms.1), calls=%async_computation.3 | async-start | bytes 2097152 | tf_op jit(solution)/shard_map/all_to_all | solution.py:212
  190.0 90.0 %all-to-all-start.4 = ((bf16[8,128,128]{2,1,0:T(8,128)(2,1)}), bf16[8,128,128]{2,1,0:T(8,128)(2,1)S(1)}, u32[]{:S(2)}, u32[]{:S(2)}) async-start(bf16[8,128,128]{2,1,0:T(8,128)(2,1)} %broadcast_in_dim.36), calls=%async_computation.4 | async-start | bytes 524288 | tf_op jit(solution)/shard_map/all_to_all | solution.py:212
  198.5 75.5 %all-reduce.3.cloned.1.call-start = ((), (), s32[]{:S(2)}) async-start(), calls=%async_computation.5 | async-start | bytes 131072 | tf_op jit(solution)/shard_map/psum | solution.py:269
Sparse Core Ops, SparseCore 0:
  202.2 71.7 all-reduce.2

commit v2 on v1

v2 whole, which is shorter than its diff:
```python
import functools
import math

import jax
import jax.numpy as jnp
from jax import lax
from jax.experimental import pallas as pl
from jax.experimental.pallas import tpu as pltpu
from jax.sharding import PartitionSpec as P

HEAD = 128
BLK = 64
VMEM_ALL = 60 << 20
TILE = 16
META = 16
BF = jnp.bfloat16
F32 = jnp.float32
NT = (((1,), (1,)), ((), ()))
TN = (((0,), (0,)), ((), ()))
NN = (((1,), (0,)), ((), ()))


def dot(a, b, dims):
    return lax.dot_general(a, b, dims, preferred_element_type=F32)


def whole(shape, space=pltpu.VMEM):
    return pl.BlockSpec(memory_space=space)


def pack_kernel(lists_ref, counts_ref, q_ref, k_ref, v_ref, g_ref, out_ref):
    rows = q_ref.shape[0]
    blocks, nbr = lists_ref.shape
    row = lax.broadcasted_iota(jnp.int32, (META, HEAD), 0)
    lane = lax.broadcasted_iota(jnp.int32, (META, HEAD), 1)
    meta = jnp.zeros((META, HEAD), jnp.int32)
    for b in range(blocks):
        for n in range(nbr + 1):
            value = counts_ref[0, b] if n == nbr else lists_ref[b, n]
            meta = jnp.where((row == b) & (lane == n), value, meta)
    meta = meta.astype(F32).astype(BF)
    for j in range(out_ref.shape[0]):
        cols = slice(j * HEAD, (j + 1) * HEAD)
        for t, ref in enumerate((q_ref, k_ref, v_ref, g_ref)):
            out_ref[j, t * rows:(t + 1) * rows, :] = ref[:, cols]
        out_ref[j, 4 * rows:, :] = meta


def pack(lists, counts, q, k, v, g, heads_per_step=16):
    rows, feats = q.shape
    heads = feats // HEAD
    out_rows = 4 * rows + META
    spec = pl.BlockSpec((rows, heads_per_step * HEAD), lambda i: (0, i))
    return pl.pallas_call(
        pack_kernel,
        grid=(heads // heads_per_step,),
        in_specs=[pl.BlockSpec(memory_space=pltpu.SMEM)] * 2 + [spec] * 4,
        out_specs=pl.BlockSpec((heads_per_step, out_rows, HEAD), lambda i: (i, 0, 0)),
        out_shape=jax.ShapeDtypeStruct((heads, out_rows, HEAD), BF),
        compiler_params=pltpu.CompilerParams(vmem_limit_bytes=VMEM_ALL),
        cost_estimate=pl.CostEstimate(flops=0, bytes_accessed=16 * rows * feats, transcendentals=0),
        name="pack",
    )(lists, counts, q, k, v, g)


def lowrank_kernel(x_ref, down_ref, out_ref):
    low = dot(x_ref[...], down_ref[...], NT).astype(BF)
    for j in range(out_ref.shape[0]):
        out_ref[j] = low


def lowrank(x, down, copies):
    rows, feats = x.shape
    return pl.pallas_call(
        lowrank_kernel,
        in_specs=[pl.BlockSpec(memory_space=pltpu.VMEM)] * 2,
        out_specs=pl.BlockSpec(memory_space=pltpu.VMEM),
        out_shape=jax.ShapeDtypeStruct((copies, rows, down.shape[0]), BF),
        compiler_params=pltpu.CompilerParams(vmem_limit_bytes=VMEM_ALL),
        cost_estimate=pl.CostEstimate(
            flops=2 * rows * feats * down.shape[0], bytes_accessed=6 * rows * feats, transcendentals=0
        ),
        name="lowrank",
    )(x, down)


def blockdiag(x):
    zero = jnp.zeros((BLK, HEAD), BF)
    upper = jnp.concatenate([x[:BLK], zero], axis=1)
    lower = jnp.concatenate([zero, x[BLK:]], axis=1)
    return jnp.concatenate([upper, lower], axis=0)


def attention_kernel(ids_ref, counts_ref, states_ref, out_ref, dq_ref, dk_ref, dv_ref, *scratch, rows, slots):
    pairs = out_ref.shape[0]
    scale = HEAD ** (-0.5)
    part_tiles, block_tiles = rows // TILE, BLK // TILE
    stride = 4 * part_tiles + META // TILE
    to_exp2 = scale * math.log2(math.e)
    s_bufs, g_bufs, w_bufs, d_bufs = (scratch[2 * i:2 * i + 2] for i in range(4))
    first_half = lax.broadcasted_iota(jnp.int32, (1, 2 * BLK), 1) < BLK

    def load(first, tiles):
        return states_ref[pl.ds(first, tiles)].reshape(tiles * TILE, HEAD)

    def of_slot(p, s):
        return [ids_ref[(2 * p + c) * slots + s] for c in range(2)]

    def own(p, part):
        return blockdiag(load(p * stride + part * part_tiles, part_tiles))

    def gathered(p, part):
        tiles = []
        for s in range(slots):
            at = [(code & 0xFFFF) + part * part_tiles for code in of_slot(p, s)]
            tiles.append(jnp.concatenate([load(a, block_tiles) for a in at], axis=1))
        return jnp.concatenate(tiles, axis=0)

    def products(p, s_buf, g_buf):
        s_buf[...] = dot(gathered(p, 1), own(p, 0), NT)
        g_buf[...] = dot(gathered(p, 2), own(p, 3), NT)

    def softmax(p, s_buf, g_buf, w_buf, d_buf):
        count = jnp.where(first_half, counts_ref[2 * p], counts_ref[2 * p + 1])
        tiles = [slice(s * BLK, (s + 1) * BLK) for s in range(slots)]
        fold = lambda op, x: functools.reduce(op, [x[r:r + 8] for r in range(0, BLK, 8)])
        top = None
        for s, at in enumerate(tiles):
            part = fold(jnp.maximum, s_buf[at, :])
            part = jnp.where(s <= count, part, -jnp.inf)
            top = part if top is None else jnp.maximum(top, part)
        top = jnp.max(top, axis=0, keepdims=True)
        total = None
        for s, at in enumerate(tiles):
            expd = jnp.exp2((s_buf[at, :] - jnp.where(s <= count, top, jnp.inf)) * to_exp2)
            s_buf[at, :] = expd
            part = fold(jnp.add, expd)
            total = part if total is None else total + part
        inverse = 1.0 / jnp.sum(total, axis=0, keepdims=True)
        delta = None
        for at in tiles:
            weights_b = (s_buf[at, :] * inverse).astype(BF)
            w_buf[at, :] = weights_b
            part = fold(jnp.add, weights_b.astype(F32) * g_buf[at, :])
            delta = part if delta is None else delta + part
        delta = jnp.sum(delta, axis=0, keepdims=True)
        for at in tiles:
            d_buf[at, :] = (s_buf[at, :] * inverse * (g_buf[at, :] - delta)).astype(BF)

    def gradients(p, w_buf, d_buf):
        q_bd = own(p, 0)
        g_bd = own(p, 3)
        dk = dot(d_buf[...], q_bd, NN)
        dv = dot(w_buf[...], g_bd, NN)
        for s in range(slots):
            for c, code in enumerate(of_slot(p, s)):
                at = code >> 16
                part = (slice(s * BLK, (s + 1) * BLK), slice(c * HEAD, (c + 1) * HEAD))
                dk_ref[at] += dk[part]
                dv_ref[at] += dv[part]
        dq = dot(d_buf[...], gathered(p, 1), TN)
        dq_ref[p, :BLK, :] = (dq[:BLK, :HEAD] * scale).astype(BF)
        dq_ref[p, BLK:, :] = (dq[BLK:, HEAD:] * scale).astype(BF)

    def step(p, c, a=True, b=True, g=True):
        if g:
            gradients(p - 2, w_bufs[c], d_bufs[c])
        if a:
            products(p, s_bufs[c], g_bufs[c])
        if b:
            softmax(p - 1, s_bufs[1 - c], g_bufs[1 - c], w_bufs[1 - c], d_bufs[1 - c])

    dk_ref[...] = jnp.zeros_like(dk_ref)
    dv_ref[...] = jnp.zeros_like(dv_ref)
    step(0, 0, b=False, g=False)
    step(1, 1, g=False)

    def body(i, carry):
        step(2 * i, 0)
        step(2 * i + 1, 1)
        return carry

    lax.fori_loop(1, pairs // 2, body, 0)
    step(pairs, 0, a=False)
    step(pairs + 1, 1, a=False, b=False)

    def finish(p, carry):
        at = pl.ds(2 * p, 2)
        out_ref[p, :rows, :] = (dk_ref[at].reshape(rows, HEAD) * scale).astype(BF)
        out_ref[p, rows:, :] = dv_ref[at].reshape(rows, HEAD).astype(BF)
        return carry

    lax.fori_loop(0, pairs, finish, 0)


def attention(ids, counts, states, rows):
    pairs = states.shape[0]
    slots = ids.shape[1]
    all_rows = pairs * rows
    stride = states.shape[1] // TILE
    ids = (ids >> 1) * stride + (ids & 1) * (BLK // TILE) | (ids << 16)
    wide = (slots * BLK, 2 * BLK)
    return pl.pallas_call(
        functools.partial(attention_kernel, rows=rows, slots=slots),
        in_specs=[
            pl.BlockSpec(memory_space=pltpu.SMEM),
            pl.BlockSpec(memory_space=pltpu.SMEM),
            pl.BlockSpec(memory_space=pltpu.VMEM),
        ],
        out_specs=[pl.BlockSpec(memory_space=pltpu.VMEM)] * 2,
        out_shape=[
            jax.ShapeDtypeStruct((pairs, 2 * rows, HEAD), BF),
            jax.ShapeDtypeStruct((pairs, rows, HEAD), BF),
        ],
        scratch_shapes=[pltpu.VMEM((all_rows // BLK, BLK, HEAD), F32)] * 2
        + [pltpu.VMEM(wide, F32)] * 4
        + [pltpu.VMEM(wide, BF)] * 4,
        compiler_params=pltpu.CompilerParams(vmem_limit_bytes=VMEM_ALL),
        cost_estimate=pl.CostEstimate(
            flops=2 * 5 * all_rows * slots * BLK * HEAD * 2,
            bytes_accessed=states.size * 2 + pairs * 3 * rows * HEAD * 2,
            transcendentals=all_rows * slots * BLK,
        ),
        name="attention",
    )(ids.reshape(-1), counts, states.reshape(-1, TILE, HEAD))


def down_kernel(grads_ref, up_ref, x_ref, out_ref):
    heads = grads_ref.shape[0]
    rows, feats = x_ref.shape
    low = []
    for t in range(2):
        total = jnp.zeros((rows, up_ref.shape[1]), F32)
        for h in range(heads):
            part = grads_ref[h, t * rows:(t + 1) * rows, :]
            total += dot(part, up_ref[t, :, h * HEAD:(h + 1) * HEAD], NT)
        low.append(total)
    back_low = jnp.concatenate(low, axis=1).astype(BF)
    for h in range(heads):
        out_ref[h] = dot(back_low, x_ref[:, h * HEAD:(h + 1) * HEAD], TN).astype(BF)


def down_terms(grads, adapter_up, x):
    heads = grads.shape[0]
    rows, feats = x.shape
    return pl.pallas_call(
        down_kernel,
        in_specs=[pl.BlockSpec(memory_space=pltpu.VMEM)] * 3,
        out_specs=pl.BlockSpec(memory_space=pltpu.VMEM),
        out_shape=jax.ShapeDtypeStruct((heads, 2 * adapter_up.shape[1], HEAD), BF),
        compiler_params=pltpu.CompilerParams(vmem_limit_bytes=VMEM_ALL),
        cost_estimate=pl.CostEstimate(
            flops=8 * rows * feats * adapter_up.shape[1],
            bytes_accessed=12 * rows * feats,
            transcendentals=0,
        ),
        name="down_terms",
    )(grads, adapter_up, x)


def unpack(grads, rows):
    parts = grads.reshape(grads.shape[0], -1, rows, HEAD)
    return [parts[:, t].transpose(1, 0, 2).reshape(rows, -1) for t in range(parts.shape[1])]


def swap(x, axis):
    return lax.all_to_all(x, axis, split_axis=0, concat_axis=0, tiled=True)


def sum_windows(x):
    n = lax.axis_size("dp")
    step = 1
    while step < n:
        x = x + lax.ppermute(x, "dp", [(i, i ^ step) for i in range(n)])
        step *= 2
    return x


def shards(
    features,
    query_states,
    key_states,
    value_states,
    cotangent,
    adapter_down,
    adapter_up,
    block_lists,
    block_counts,
):
    zones = lax.axis_size("zone")
    windows = lax.axis_size("dp")
    rows = query_states.shape[1]
    rank = adapter_down.shape[1]
    all_rows = zones * rows
    blocks = all_rows // BLK
    own_blocks = rows // BLK
    nbr = block_lists.shape[2]
    x = features[0]

    sent = pack(
        block_lists[0], block_counts, query_states[0], key_states[0], value_states[0], cotangent[0]
    )
    states = swap(sent, "zone")

    info = states[:, 4 * rows:4 * rows + own_blocks, :nbr + 1].astype(jnp.int32)
    info = info.reshape(blocks, nbr + 1)
    counts = info[:, nbr]
    own = jnp.arange(blocks, dtype=jnp.int32)[:, None]
    slot = jnp.arange(nbr, dtype=jnp.int32)[None, :]
    ids = jnp.concatenate([own, jnp.where(slot < counts[:, None], info[:, :nbr], own)], axis=1)

    low = lowrank(x, adapter_down.reshape(2 * rank, -1), zones)
    low, states = lax.optimization_barrier((low, states))
    low_all = swap(low, "zone")

    grads, dq = attention(ids, counts, states, rows)
    grads, low_all = lax.optimization_barrier((grads, low_all))
    home = swap(grads, "zone")

    stacked = grads.reshape(zones, 2, rows, HEAD)
    up = jnp.concatenate(
        [
            jnp.einsum(
                "zra,zrf->af",
                low_all[:, :, t * rank:(t + 1) * rank],
                stacked[:, t],
                preferred_element_type=F32,
            )
            for t in range(2)
        ]
    )
    up = sum_windows(up)

    terms, up = lax.optimization_barrier((down_terms(home, adapter_up, x), up))
    terms = swap(terms, "zone")
    key_grad, value_grad = unpack(home, rows)
    dq, terms, key_grad, value_grad = lax.optimization_barrier((dq, terms, key_grad, value_grad))
    dq = swap(dq, "zone")
    down = sum_windows(jnp.sum(terms.astype(F32), axis=0))
    (query_grad,) = unpack(dq, rows)
    factor = 1.0 / math.sqrt(windows * all_rows)
    return (
        query_grad[None],
        key_grad[None],
        value_grad[None],
        down.reshape(2, rank, HEAD) * factor,
        up.reshape(2, rank, HEAD) * factor,
    )


def solution(mesh):
    rows = P("dp", "zone", None)
    cols = P(None, None, "zone")
    in_specs = (rows, rows, rows, rows, rows, P(), P(), rows, P("dp", "zone"))
    out_specs = (rows, rows, rows, cols, cols)
    return jax.shard_map(shards, mesh=mesh, in_specs=in_specs, out_specs=out_specs, check_vma=False)
```

time: 288 us -> 186 us (0.65)
  waiting for transfers between devices: 138 us -> 79.4 us
  blocking collectives: 44.4 us -> 0 us
  starting transfers between devices: 31.7 us -> 62.3 us
  Pallas kernels: 47 us -> 32.2 us
  between operations: 14.1 us -> 0.78 us
  other arithmetic: 5.08 us -> 1.52 us
  local copies, waits for them, and re-layouts: 4.07 us -> 7.06 us
    psum x1 -> x0, waiting for transfers between devices: 73.2 us -> none  [shards(): up = lax.psum(up, 'dp')]
    all_to_all x1 -> x0, blocking collectives: 44.4 us -> none  [swap(): return lax.all_to_all(x, axis, split_axis=0, concat_axis=0, tiled=True)]
    ppermute x0 -> x6, starting transfers between devices: none -> 24.9 us  [sum_windows(): x = x + lax.ppermute(x, 'dp', [(i, i ^ step) for i in range(n)])]
    ppermute x0 -> x6, waiting for transfers between devices: none -> 14.4 us  [sum_windows(): x = x + lax.ppermute(x, 'dp', [(i, i ^ step) for i in range(n)])]
    pallas_call x1, Pallas kernels: 32.8 us -> 20.8 us  [attention(): pl.pallas_call(functools.partial(attention_kernel, rows=rows, slots=slots...]
    all_to_all x4 -> x5, starting transfers between devices: 31.7 us -> 37.4 us  [swap(): return lax.all_to_all(x, axis, split_axis=0, concat_axis=0, tiled=True)]
    all_to_all x4 -> x5, waiting for transfers between devices: 64.3 us -> 65 us  [swap(): return lax.all_to_all(x, axis, split_axis=0, concat_axis=0, tiled=True)]
  transfers between devices with their start and end apart: 5 -> 11, of which waited for: 3 -> 9; matrix products, arithmetic and copies ran while one was open for 3% -> 4% of each run, Pallas kernels for 13% -> 13%
where the time goes in v2:
time: 186 us
  waiting for transfers between devices  79.4 us (43%)
  starting transfers between devices  62.3 us (33%)
  Pallas kernels  32.2 us (17%)
  local copies, waits for them, and re-layouts  7.06 us (4%)
  matrix products  2.55 us (1%)
    all_to_all x5, waiting for transfers between devices, swap(): return lax.all_to_all(x, axis, split_axis=0, concat_axis=0, tiled=True)  65 us
    all_to_all x5, starting transfers between devices, swap(): return lax.all_to_all(x, axis, split_axis=0, concat_axis=0, tiled=True)  37.4 us
    ppermute x6, starting transfers between devices, sum_windows(): x = x + lax.ppermute(x, 'dp', [(i, i ^ step) for i in range(n)])  24.9 us
    pallas_call x1, Pallas kernels, attention(): pl.pallas_call(functools.partial(attention_kernel, rows=rows, slots=slots...  20.8 us
    ppermute x6, waiting for transfers between devices, sum_windows(): x = x + lax.ppermute(x, 'dp', [(i, i ^ step) for i in range(n)])  14.4 us
    pallas_call x1, Pallas kernels, down_terms(): pl.pallas_call(down_kernel, in_specs=[pl.BlockSpec(memory_space=pltpu.VME...  4.38 us
    pallas_call x1, Pallas kernels, pack(): pl.pallas_call(pack_kernel, grid=(heads // heads_per_step,), in_specs=[pl...  3.99 us
  transfers between devices with their start and end apart: 11, of which 9 were waited for; matrix products, arithmetic and copies ran while one was open for 4% of the time, Pallas kernels for 13%

profile of v2, /device:TPU:2, one launch (start us, length us, event | category | flops | bytes accessed | tf_op | source)
XLA Modules:
  0.0 185.7 jit_solution(17351294451931937830)
XLA Ops:
  0.6 4.0 %pack.1 = bf16[32,528,128]{2,1,0:T(8,128)(2,1)} custom-call(s32[2,8]{1,0:T(2,128)} %bitcast.68, s32[1,2]{1,0:T(1,128)} %counts_ref.1, bf16[128,4096]{1,0:T(8,128)(2,1)} %bitcast.55, bf16[128,4096]{1,0:T(8,128)(2,1)} %bitcast.56, bf16[128,4096]{1,0:T(8,128)(2,1)} %bitcast.57, bf16[128,4096]{1,0:T(8,128)(2,1)} %bitcast.58), custom_call_target="tpu_custom_call" | custom-call | bytes 8388608 | tf_op jit(solution)/shard_map/pack/pallas_call | solution.py:54
  4.6 7.7 %all-to-all-start = ((bf16[32,528,128]{2,1,0:T(8,128)(2,1)}), bf16[32,528,128]{2,1,0:T(8,128)(2,1)}, u32[]{:S(2)}, u32[]{:S(2)}) async-start(bf16[32,528,128]{2,1,0:T(8,128)(2,1)} %pack.1), calls=%async_computation | async-start | bytes 8650752 | tf_op jit(solution)/shard_map/all_to_all | solution.py:267
  12.3 3.0 %lowrank.1 = bf16[32,128,128]{2,1,0:T(8,128)(2,1)} custom-call(bf16[128,4096]{1,0:T(8,128)(2,1)} %bitcast.49, bf16[128,4096]{1,0:T(8,128)(2,1)} %bitcast.59), custom_call_target="tpu_custom_call" | custom-call | flops 134217728 | bytes 3145728 | tf_op jit(solution)/shard_map/lowrank/pallas_call | solution.py:74
  15.3 49.0 %all-to-all-done = bf16[32,528,128]{2,1,0:T(8,128)(2,1)} async-done(((bf16[32,528,128]{2,1,0:T(8,128)(2,1)}), bf16[32,528,128]{2,1,0:T(8,128)(2,1)}, u32[]{:S(2)}, u32[]{:S(2)}) %all-to-all-start) | async-done | bytes 4325408 | tf_op jit(solution)/shard_map/all_to_all | solution.py:267
  64.3 9.0 %all-to-all-start.1 = ((bf16[32,128,128]{2,1,0:T(8,128)(2,1)}), bf16[32,128,128]{2,1,0:T(8,128)(2,1)S(1)}, u32[]{:S(2)}, u32[]{:S(2)}) async-start(bf16[32,128,128]{2,1,0:T(8,128)(2,1)} %lowrank.1), calls=%async_computation.1 | async-start | bytes 2097152 | tf_op jit(solution)/shard_map/all_to_all | solution.py:267
  73.3 0.9 slice.36
  74.5 0.7 or.8.ids_ref
  75.3 20.8 %attention.1 = (bf16[32,256,128]{2,1,0:T(8,128)(2,1)}, bf16[32,128,128]{2,1,0:T(8,128)(2,1)}) custom-call(s32[576]{0:T(1024)} %or.8.ids_ref, s32[64]{0:T(128)} %bitcast.67, bf16[1056,16,128]{2,1,0:T(8,128)(2,1)} %bitcast.10.states_ref), custom_call_target="tpu_custom_call" | custom-call | flops 6039797760 | bytes 7471104 | tf_op jit(solution)/shard_map/attention/pallas_call | solution.py:203
  96.1 7.4 %all-to-all-start.2 = ((bf16[32,256,128]{2,1,0:T(8,128)(2,1)}), bf16[32,256,128]{2,1,0:T(8,128)(2,1)S(1)}, u32[]{:S(2)}, u32[]{:S(2)}) async-start(bf16[32,256,128]{2,1,0:T(8,128)(2,1)} %get-tuple-element.21), calls=%async_computation.2 | async-start | bytes 4194304 | tf_op jit(solution)/shard_map/all_to_all | solution.py:267
  103.5 1.8 convolution_bitcast_fusion.1
  105.4 0.7 convolution_bitcast_fusion
  106.1 2.0 %collective-permute-start = (f32[128,128]{1,0:T(8,128)S(1)}, f32[128,128]{1,0:T(8,128)S(1)}, u32[]{:S(2)}, u32[]{:S(2)}) collective-permute-start(f32[128,128]{1,0:T(8,128)S(1)} %pad_maximum_fusion), channel_id=1, source_target_pairs={{0,32},{32,0},{64,96},{96,64},{128,160},{160,128},{192,224},{224,1... | collective-permute-start | bytes 196616 | tf_op jit(solution)/shard_map/ppermute | solution.py:274
  108.1 2.4 %collective-permute-done = f32[128,128]{1,0:T(8,128)S(1)} collective-permute-done((f32[128,128]{1,0:T(8,128)S(1)}, f32[128,128]{1,0:T(8,128)S(1)}, u32[]{:S(2)}, u32[]{:S(2)}) %collective-permute-start) | collective-permute-done | bytes 65568 | tf_op jit(solution)/shard_map/ppermute | solution.py:274
  110.6 3.3 %collective-permute-start.1 = (f32[128,128]{1,0:T(8,128)S(1)}, f32[128,128]{1,0:T(8,128)S(1)}, u32[]{:S(2)}, u32[]{:S(2)}) collective-permute-start(f32[128,128]{1,0:T(8,128)S(1)} %fusion.9), channel_id=1, source_target_pairs={{0,64},{32,96},{64,0},{96,32},{128,192},{160,224},{192,128},{224,1... | collective-permute-start | bytes 196616 | tf_op jit(solution)/shard_map/ppermute | solution.py:274
  113.9 2.9 %collective-permute-done.1 = f32[128,128]{1,0:T(8,128)S(1)} collective-permute-done((f32[128,128]{1,0:T(8,128)S(1)}, f32[128,128]{1,0:T(8,128)S(1)}, u32[]{:S(2)}, u32[]{:S(2)}) %collective-permute-start.1) | collective-permute-done | bytes 65568 | tf_op jit(solution)/shard_map/ppermute | solution.py:274
  116.8 7.1 %collective-permute-start.2 = (f32[128,128]{1,0:T(8,128)S(1)}, f32[128,128]{1,0:T(8,128)S(1)}, u32[]{:S(2)}, u32[]{:S(2)}) collective-permute-start(f32[128,128]{1,0:T(8,128)S(1)} %add.25), channel_id=1, source_target_pairs={{0,128},{32,160},{64,192},{96,224},{128,0},{160,32},{192,64},{224,... | collective-permute-start | bytes 196616 | tf_op jit(solution)/shard_map/ppermute | solution.py:274
  123.8 2.2 %collective-permute-done.2 = f32[128,128]{1,0:T(8,128)S(1)} collective-permute-done((f32[128,128]{1,0:T(8,128)S(1)}, f32[128,128]{1,0:T(8,128)S(1)}, u32[]{:S(2)}, u32[]{:S(2)}) %collective-permute-start.2) | collective-permute-done | bytes 65568 | tf_op jit(solution)/shard_map/ppermute | solution.py:274
  126.1 3.3 %all-to-all-done.2.grads_ref = bf16[32,256,128]{2,1,0:T(8,128)(2,1)S(1)} async-done(((bf16[32,256,128]{2,1,0:T(8,128)(2,1)}), bf16[32,256,128]{2,1,0:T(8,128)(2,1)S(1)}, u32[]{:S(2)}, u32[]{:S(2)}) %all-to-all-start.2) | async-done | bytes 2097184 | tf_op jit(solution)/shard_map/all_to_all | solution.py:267
  129.4 1.3 copy-done
  130.7 4.4 %down_terms.1 = bf16[32,128,128]{2,1,0:T(8,128)(2,1)} custom-call(bf16[32,256,128]{2,1,0:T(8,128)(2,1)} %copy-done, bf16[2,64,4096]{2,1,0:T(8,128)(2,1)} %up_ref.1, bf16[128,4096]{1,0:T(8,128)(2,1)} %bitcast.50), custom_call_target="tpu_custom_call" | custom-call | flops 268435456 | bytes 6291456 | tf_op jit(solution)/shard_map/down_terms/pallas_call | solution.py:246
  135.1 7.0 %all-to-all-start.3 = ((bf16[32,128,128]{2,1,0:T(8,128)(2,1)}), bf16[32,128,128]{2,1,0:T(8,128)(2,1)S(1)}, u32[]{:S(2)}, u32[]{:S(2)}) async-start(bf16[32,128,128]{2,1,0:T(8,128)(2,1)} %down_terms.1), calls=%async_computation.3 | async-start | bytes 2097152 | tf_op jit(solution)/shard_map/all_to_all | solution.py:267
  142.3 1.6 copy_bitcast_fusion
  143.9 12.7 %all-to-all-done.3 = bf16[32,128,128]{2,1,0:T(8,128)(2,1)S(1)} async-done(((bf16[32,128,128]{2,1,0:T(8,128)(2,1)}), bf16[32,128,128]{2,1,0:T(8,128)(2,1)S(1)}, u32[]{:S(2)}, u32[]{:S(2)}) %all-to-all-start.3) | async-done | bytes 1048608 | tf_op jit(solution)/shard_map/all_to_all | solution.py:267
  156.6 6.4 %all-to-all-start.4 = ((bf16[32,128,128]{2,1,0:T(8,128)(2,1)}), bf16[32,128,128]{2,1,0:T(8,128)(2,1)S(1)}, u32[]{:S(2)}, u32[]{:S(2)}) async-start(bf16[32,128,128]{2,1,0:T(8,128)(2,1)} %get-tuple-element.24), calls=%async_computation.4 | async-start | bytes 2097152 | tf_op jit(solution)/shard_map/all_to_all | solution.py:267
  163.2 2.0 %collective-permute-start.3 = (f32[128,128]{1,0:T(8,128)S(1)}, f32[128,128]{1,0:T(8,128)S(1)}, u32[]{:S(2)}, u32[]{:S(2)}) collective-permute-start(f32[128,128]{1,0:T(8,128)S(1)} %convert_reduce_fusion), channel_id=1, source_target_pairs={{0,32},{32,0},{64,96},{96,64},{128,160},{160,128},{192,224},{224,1... | collective-permute-start | bytes 196616 | tf_op jit(solution)/shard_map/ppermute | solution.py:274
  165.2 2.4 %collective-permute-done.3 = f32[128,128]{1,0:T(8,128)S(1)} collective-permute-done((f32[128,128]{1,0:T(8,128)S(1)}, f32[128,128]{1,0:T(8,128)S(1)}, u32[]{:S(2)}, u32[]{:S(2)}) %collective-permute-start.3) | collective-permute-done | bytes 65568 | tf_op jit(solution)/shard_map/ppermute | solution.py:274
  167.6 3.3 %collective-permute-start.4 = (f32[128,128]{1,0:T(8,128)S(1)}, f32[128,128]{1,0:T(8,128)S(1)}, u32[]{:S(2)}, u32[]{:S(2)}) collective-permute-start(f32[128,128]{1,0:T(8,128)S(1)} %add.27), channel_id=1, source_target_pairs={{0,64},{32,96},{64,0},{96,32},{128,192},{160,224},{192,128},{224,1... | collective-permute-start | bytes 196616 | tf_op jit(solution)/shard_map/ppermute | solution.py:274
  170.9 2.9 %collective-permute-done.4 = f32[128,128]{1,0:T(8,128)S(1)} collective-permute-done((f32[128,128]{1,0:T(8,128)S(1)}, f32[128,128]{1,0:T(8,128)S(1)}, u32[]{:S(2)}, u32[]{:S(2)}) %collective-permute-start.4) | collective-permute-done | bytes 65568 | tf_op jit(solution)/shard_map/ppermute | solution.py:274
  173.8 7.1 %collective-permute-start.5 = (f32[128,128]{1,0:T(8,128)S(1)}, f32[128,128]{1,0:T(8,128)S(1)}, u32[]{:S(2)}, u32[]{:S(2)}) collective-permute-start(f32[128,128]{1,0:T(8,128)S(1)} %add.28), channel_id=1, source_target_pairs={{0,128},{32,160},{64,192},{96,224},{128,0},{160,32},{192,64},{224,... | collective-permute-start | bytes 196616 | tf_op jit(solution)/shard_map/ppermute | solution.py:274
  181.5 1.6 collective-permute-done.5
  183.8 0.7 copy.46
  184.4 1.3 copy.47
  (27 shorter events, 2.1 us)
Async XLA Ops:
  4.6 59.7 %all-to-all-start = ((bf16[32,528,128]{2,1,0:T(8,128)(2,1)}), bf16[32,528,128]{2,1,0:T(8,128)(2,1)}, u32[]{:S(2)}, u32[]{:S(2)}) async-start(bf16[32,528,128]{2,1,0:T(8,128)(2,1)} %pack.1), calls=%async_computation | async-start | bytes 8650752 | tf_op jit(solution)/shard_map/all_to_all | solution.py:267
  64.3 31.7 %all-to-all-start.1 = ((bf16[32,128,128]{2,1,0:T(8,128)(2,1)}), bf16[32,128,128]{2,1,0:T(8,128)(2,1)S(1)}, u32[]{:S(2)}, u32[]{:S(2)}) async-start(bf16[32,128,128]{2,1,0:T(8,128)(2,1)} %lowrank.1), calls=%async_computation.1 | async-start | bytes 2097152 | tf_op jit(solution)/shard_map/all_to_all | solution.py:267
  74.3 0.9 copy-start.3
  96.1 33.3 %all-to-all-start.2 = ((bf16[32,256,128]{2,1,0:T(8,128)(2,1)}), bf16[32,256,128]{2,1,0:T(8,128)(2,1)S(1)}, u32[]{:S(2)}, u32[]{:S(2)}) async-start(bf16[32,256,128]{2,1,0:T(8,128)(2,1)} %get-tuple-element.21), calls=%async_computation.2 | async-start | bytes 4194304 | tf_op jit(solution)/shard_map/all_to_all | solution.py:267
  103.5 1.9 %copy-start.2 = (bf16[32,256,128]{2,1,0:T(8,128)(2,1)S(1)}, bf16[32,256,128]{2,1,0:T(8,128)(2,1)}, u32[]{:S(2)}) copy-start(bf16[32,256,128]{2,1,0:T(8,128)(2,1)} %get-tuple-element.21) | copy-start | bytes 6291460
  106.1 4.4 %collective-permute-start = (f32[128,128]{1,0:T(8,128)S(1)}, f32[128,128]{1,0:T(8,128)S(1)}, u32[]{:S(2)}, u32[]{:S(2)}) collective-permute-start(f32[128,128]{1,0:T(8,128)S(1)} %pad_maximum_fusion), channel_id=1, source_target_pairs={{0,32},{32,0},{64,96},{96,64},{128,160},{160,128},{192,224},{224,1... | collective-permute-start | bytes 196616 | tf_op jit(solution)/shard_map/ppermute | solution.py:274
  110.6 6.2 %collective-permute-start.1 = (f32[128,128]{1,0:T(8,128)S(1)}, f32[128,128]{1,0:T(8,128)S(1)}, u32[]{:S(2)}, u32[]{:S(2)}) collective-permute-start(f32[128,128]{1,0:T(8,128)S(1)} %fusion.9), channel_id=1, source_target_pairs={{0,64},{32,96},{64,0},{96,32},{128,192},{160,224},{192,128},{224,1... | collective-permute-start | bytes 196616 | tf_op jit(solution)/shard_map/ppermute | solution.py:274
  116.8 9.3 %collective-permute-start.2 = (f32[128,128]{1,0:T(8,128)S(1)}, f32[128,128]{1,0:T(8,128)S(1)}, u32[]{:S(2)}, u32[]{:S(2)}) collective-permute-start(f32[128,128]{1,0:T(8,128)S(1)} %add.25), channel_id=1, source_target_pairs={{0,128},{32,160},{64,192},{96,224},{128,0},{160,32},{192,64},{224,... | collective-permute-start | bytes 196616 | tf_op jit(solution)/shard_map/ppermute | solution.py:274
  129.4 1.3 copy-start
  135.1 7.0 %copy-start.1 = (bf16[32,256,128]{2,1,0:T(8,128)(2,1)S(1)}, bf16[32,256,128]{2,1,0:T(8,128)(2,1)}, u32[]{:S(2)}) copy-start(bf16[32,256,128]{2,1,0:T(8,128)(2,1)} %copy-done) | copy-start | bytes 6291460
  135.1 21.5 %all-to-all-start.3 = ((bf16[32,128,128]{2,1,0:T(8,128)(2,1)}), bf16[32,128,128]{2,1,0:T(8,128)(2,1)S(1)}, u32[]{:S(2)}, u32[]{:S(2)}) async-start(bf16[32,128,128]{2,1,0:T(8,128)(2,1)} %down_terms.1), calls=%async_computation.3 | async-start | bytes 2097152 | tf_op jit(solution)/shard_map/all_to_all | solution.py:267
  156.6 27.2 %all-to-all-start.4 = ((bf16[32,128,128]{2,1,0:T(8,128)(2,1)}), bf16[32,128,128]{2,1,0:T(8,128)(2,1)S(1)}, u32[]{:S(2)}, u32[]{:S(2)}) async-start(bf16[32,128,128]{2,1,0:T(8,128)(2,1)} %get-tuple-element.24), calls=%async_computation.4 | async-start | bytes 2097152 | tf_op jit(solution)/shard_map/all_to_all | solution.py:267
  163.2 4.4 %collective-permute-start.3 = (f32[128,128]{1,0:T(8,128)S(1)}, f32[128,128]{1,0:T(8,128)S(1)}, u32[]{:S(2)}, u32[]{:S(2)}) collective-permute-start(f32[128,128]{1,0:T(8,128)S(1)} %convert_reduce_fusion), channel_id=1, source_target_pairs={{0,32},{32,0},{64,96},{96,64},{128,160},{160,128},{192,224},{224,1... | collective-permute-start | bytes 196616 | tf_op jit(solution)/shard_map/ppermute | solution.py:274
  167.6 6.2 %collective-permute-start.4 = (f32[128,128]{1,0:T(8,128)S(1)}, f32[128,128]{1,0:T(8,128)S(1)}, u32[]{:S(2)}, u32[]{:S(2)}) collective-permute-start(f32[128,128]{1,0:T(8,128)S(1)} %add.27), channel_id=1, source_target_pairs={{0,64},{32,96},{64,0},{96,32},{128,192},{160,224},{192,128},{224,1... | collective-permute-start | bytes 196616 | tf_op jit(solution)/shard_map/ppermute | solution.py:274
  173.8 9.3 %collective-permute-start.5 = (f32[128,128]{1,0:T(8,128)S(1)}, f32[128,128]{1,0:T(8,128)S(1)}, u32[]{:S(2)}, u32[]{:S(2)}) collective-permute-start(f32[128,128]{1,0:T(8,128)S(1)} %add.28), channel_id=1, source_target_pairs={{0,128},{32,160},{64,192},{96,224},{128,0},{160,32},{192,64},{224,... | collective-permute-start | bytes 196616 | tf_op jit(solution)/shard_map/ppermute | solution.py:274

commit v3 on v2

v3 whole, which is shorter than its diff:
```python
import functools
import math

import jax
import jax.numpy as jnp
from jax import lax
from jax.experimental import pallas as pl
from jax.experimental.pallas import tpu as pltpu
from jax.sharding import PartitionSpec as P

HEAD = 128
BLK = 64
VMEM_ALL = 63 << 20
TILE = 16
LIST = 16
META = 16
BF = jnp.bfloat16
F32 = jnp.float32
NT = (((1,), (1,)), ((), ()))
TN = (((0,), (0,)), ((), ()))
NN = (((1,), (0,)), ((), ()))


def dot(a, b, dims):
    return lax.dot_general(a, b, dims, preferred_element_type=F32)


def whole(shape, space=pltpu.VMEM):
    return pl.BlockSpec(memory_space=space)


def pack_kernel(lists_ref, counts_ref, q_ref, k_ref, v_ref, g_ref, out_ref):
    rows = q_ref.shape[0]
    blocks, nbr = lists_ref.shape
    row = lax.broadcasted_iota(jnp.int32, (META, HEAD), 0)
    lane = lax.broadcasted_iota(jnp.int32, (META, HEAD), 1)
    meta = jnp.zeros((META, HEAD), jnp.int32)
    for b in range(blocks):
        for n in range(nbr + 1):
            value = lists_ref[b, n - 1] if n else counts_ref[0, b]
            meta = jnp.where((row == 0) & (lane == b * LIST + n), value, meta)
    meta = meta.astype(F32).astype(BF)
    for j in range(out_ref.shape[0]):
        cols = slice(j * HEAD, (j + 1) * HEAD)
        for t, ref in enumerate((q_ref, k_ref, v_ref, g_ref)):
            out_ref[j, t * rows:(t + 1) * rows, :] = ref[:, cols]
        out_ref[j, 4 * rows:, :] = meta


def pack(lists, counts, q, k, v, g, heads_per_step=16):
    rows, feats = q.shape
    heads = feats // HEAD
    out_rows = 4 * rows + META
    spec = pl.BlockSpec((rows, heads_per_step * HEAD), lambda i: (0, i))
    return pl.pallas_call(
        pack_kernel,
        grid=(heads // heads_per_step,),
        in_specs=[pl.BlockSpec(memory_space=pltpu.SMEM)] * 2 + [spec] * 4,
        out_specs=pl.BlockSpec((heads_per_step, out_rows, HEAD), lambda i: (i, 0, 0)),
        out_shape=jax.ShapeDtypeStruct((heads, out_rows, HEAD), BF),
        compiler_params=pltpu.CompilerParams(vmem_limit_bytes=VMEM_ALL),
        cost_estimate=pl.CostEstimate(flops=0, bytes_accessed=16 * rows * feats, transcendentals=0),
        name="pack",
    )(lists, counts, q, k, v, g)


def lowrank_kernel(x_ref, down_ref, out_ref):
    low = dot(x_ref[...], down_ref[...], NT).astype(BF)
    for j in range(out_ref.shape[0]):
        out_ref[j] = low


def lowrank(x, down, copies):
    rows, feats = x.shape
    return pl.pallas_call(
        lowrank_kernel,
        in_specs=[pl.BlockSpec(memory_space=pltpu.VMEM)] * 2,
        out_specs=pl.BlockSpec(memory_space=pltpu.VMEM),
        out_shape=jax.ShapeDtypeStruct((copies, rows, down.shape[0]), BF),
        compiler_params=pltpu.CompilerParams(vmem_limit_bytes=VMEM_ALL),
        cost_estimate=pl.CostEstimate(
            flops=2 * rows * feats * down.shape[0], bytes_accessed=6 * rows * feats, transcendentals=0
        ),
        name="lowrank",
    )(x, down)


def blockdiag(x):
    zero = jnp.zeros((BLK, HEAD), BF)
    upper = jnp.concatenate([x[:BLK], zero], axis=1)
    lower = jnp.concatenate([zero, x[BLK:]], axis=1)
    return jnp.concatenate([upper, lower], axis=0)


def attention_kernel(
    states_hbm,
    out_hbm,
    dq_hbm,
    states_ref,
    out_ref,
    dq_ref,
    dk_ref,
    dv_ref,
    meta_ref,
    codes_ref,
    ids_ref,
    offset_ref,
    order_ref,
    sems,
    *scratch,
    slots,
):
    blocks = dk_ref.shape[0]
    pairs = blocks // 2
    stride = states_hbm.shape[1]
    block_tiles = BLK // TILE
    part_tiles = 2 * block_tiles
    least = 2
    scale = HEAD ** (-0.5)
    to_exp2 = scale * math.log2(math.e)
    s_bufs, g_bufs, w_bufs, d_bufs = (scratch[2 * i:2 * i + 2] for i in range(4))
    first_half = lax.broadcasted_iota(jnp.int32, (1, 2 * BLK), 1) < BLK

    copy_meta = pltpu.make_async_copy(states_hbm.at[:, stride - 1], meta_ref, sems.at[0])
    copy_meta.start()
    copy_states = pltpu.make_async_copy(states_hbm, states_ref, sems.at[1])
    copy_states.start()
    dk_ref[...] = jnp.zeros_like(dk_ref)
    dv_ref[...] = jnp.zeros_like(dv_ref)

    copy_meta.wait()
    info = jnp.sum(meta_ref[...].astype(F32), axis=1).astype(jnp.int32)
    lane = lax.broadcasted_iota(jnp.int32, info.shape, 1)
    row = lax.broadcasted_iota(jnp.int32, info.shape, 0)
    second = lane >= LIST
    counts = [info[:, c * LIST:c * LIST + 1] for c in range(2)]
    count = jnp.where(second, counts[1], counts[0])
    slot = lane & (LIST - 1)
    ids = jnp.where((slot >= 1) & (slot <= count), info, 2 * row + jnp.where(second, 1, 0))
    codes = (ids >> 1) * stride + (ids & 1) * block_tiles | (ids << 16)
    for c in range(2):
        codes = jnp.where(lane == 2 * LIST + c, counts[c], codes)
    codes_ref[...] = codes
    copy_codes = pltpu.make_async_copy(codes_ref, ids_ref, sems.at[2])
    copy_codes.start()
    copy_codes.wait()

    def count_of(b):
        return ids_ref[b // 2, 2 * LIST + b % 2]

    for c in range(slots + 1):
        offset_ref[c] = 0
    for b in range(blocks):
        n = count_of(b)
        offset_ref[n] = offset_ref[n] + 1
    above = [None] * (slots + 1)
    total = 0
    for c in range(slots - 1, least - 1, -1):
        above[c] = total
        total = total + offset_ref[c]
        offset_ref[c] = above[c]
    for b in range(blocks):
        n = count_of(b)
        place = offset_ref[n]
        offset_ref[n] = place + 1
        order_ref[place] = b
    copy_states.wait()

    flat_ref = states_ref.reshape(pairs * stride, TILE, HEAD)

    def load(first, tiles):
        return flat_ref[pl.ds(first, tiles)].reshape(tiles * TILE, HEAD)

    def place_of(p):
        return [(b >> 1, b & 1) for b in (order_ref[2 * p + c] for c in range(2))]

    def of_slot(at, s):
        return [ids_ref[d, c * LIST + s] for d, c in at]

    def own(at, part):
        tiles = [load(d * stride + c * block_tiles + part * part_tiles, block_tiles) for d, c in at]
        return blockdiag(jnp.concatenate(tiles, axis=0))

    def gathered(at, part, n):
        tiles = []
        for s in range(n):
            first = [(code & 0xFFFF) + part * part_tiles for code in of_slot(at, s)]
            tiles.append(jnp.concatenate([load(f, block_tiles) for f in first], axis=1))
        return jnp.concatenate(tiles, axis=0)

    def products(p, n, s_buf, g_buf):
        at = place_of(p)
        s_buf[:n * BLK, :] = dot(gathered(at, 1, n), own(at, 0), NT)
        g_buf[:n * BLK, :] = dot(gathered(at, 2, n), own(at, 3), NT)

    def softmax(p, n, s_buf, g_buf, w_buf, d_buf):
        used = [ids_ref[d, 2 * LIST + c] for d, c in place_of(p)]
        count = jnp.where(first_half, used[0], used[1])
        tiles = [slice(s * BLK, (s + 1) * BLK) for s in range(n)]

        def fold(op, x):
            return functools.reduce(op, [x[r:r + 8] for r in range(0, BLK, 8)])

        top = None
        for s, at in enumerate(tiles):
            part = fold(jnp.maximum, s_buf[at, :])
            part = part if s <= least else jnp.where(s <= count, part, -jnp.inf)
            top = part if top is None else jnp.maximum(top, part)
        top = jnp.max(top, axis=0, keepdims=True)
        total = None
        for s, at in enumerate(tiles):
            shift = top if s <= least else jnp.where(s <= count, top, jnp.inf)
            expd = jnp.exp2((s_buf[at, :] - shift) * to_exp2)
            s_buf[at, :] = expd
            part = fold(jnp.add, expd)
            total = part if total is None else total + part
        inverse = 1.0 / jnp.sum(total, axis=0, keepdims=True)
        delta = None
        for at in tiles:
            weights_b = (s_buf[at, :] * inverse).astype(BF)
            w_buf[at, :] = weights_b
            part = fold(jnp.add, weights_b.astype(F32) * g_buf[at, :])
            delta = part if delta is None else delta + part
        delta = jnp.sum(delta, axis=0, keepdims=True)
        for at in tiles:
            d_buf[at, :] = (s_buf[at, :] * inverse * (g_buf[at, :] - delta)).astype(BF)

    def gradients(p, n, w_buf, d_buf):
        at = place_of(p)
        grad_scores = d_buf[:n * BLK, :]
        dk = dot(grad_scores, own(at, 0), NN)
        dv = dot(w_buf[:n * BLK, :], own(at, 3), NN)
        for s in range(n):
            for c, code in enumerate(of_slot(at, s)):
                block = code >> 16
                part = (slice(s * BLK, (s + 1) * BLK), slice(c * HEAD, (c + 1) * HEAD))
                dk_ref[block] += dk[part]
                dv_ref[block] += dv[part]
        dq = dot(grad_scores, gathered(at, 1, n), TN)
        for c, (d, half) in enumerate(at):
            part = dq[c * BLK:(c + 1) * BLK, c * HEAD:(c + 1) * HEAD]
            dq_ref[2 * d + half] = (part * scale).astype(BF)

    def step(p, c, n):
        gradients(p - 2, n, w_bufs[c], d_bufs[c])
        products(jnp.minimum(p, pairs - 1), n, s_bufs[c], g_bufs[c])
        softmax(
            jnp.minimum(p - 1, pairs - 1), n, s_bufs[1 - c], g_bufs[1 - c], w_bufs[1 - c], d_bufs[1 - c]
        )

    products(0, slots, s_bufs[0], g_bufs[0])
    products(1, slots, s_bufs[1], g_bufs[1])
    softmax(0, slots, s_bufs[0], g_bufs[0], w_bufs[0], d_bufs[0])
    first, last = 1, pairs // 2 + 1
    for n in range(slots, least, -1):

        def body(i, carry, n=n):
            step(2 * i, 0, n)
            step(2 * i + 1, 1, n)
            return carry

        until = last
        if n > least + 1:
            until = jnp.minimum(1 + ((above[n - 2] + 3) >> 2), last)
        lax.fori_loop(first, until, body, 0)
        first = until

    copy_dq = pltpu.make_async_copy(dq_ref, dq_hbm, sems.at[3])
    copy_dq.start()
    chunk = blocks // 4
    copies = []
    for start in range(0, blocks, chunk):

        def finish(b, carry):
            half = pl.ds(pl.multiple_of((b & 1) * BLK, BLK), BLK)
            out_ref[b >> 1, 0, half, :] = (dk_ref[b] * scale).astype(BF)
            out_ref[b >> 1, 1, half, :] = dv_ref[b].astype(BF)
            return carry

        lax.fori_loop(start, start + chunk, finish, 0, unroll=4)
        at = pl.ds(start // 2, chunk // 2)
        copies.append(
            pltpu.make_async_copy(out_ref.at[at], out_hbm.at[at], sems.at[4 + start // chunk])
        )
        copies[-1].start()
    copy_dq.wait()
    for copy in copies:
        copy.wait()


def attention(states, rows, slots):
    pairs = states.shape[0]
    blocks = pairs * rows // BLK
    tiles = states.shape[1] // TILE
    wide = (slots * BLK, 2 * BLK)
    out_shape = [
        jax.ShapeDtypeStruct((pairs, 2, rows, HEAD), BF),
        jax.ShapeDtypeStruct((blocks, BLK, HEAD), BF),
    ]
    grads, dq = pl.pallas_call(
        functools.partial(attention_kernel, slots=slots),
        in_specs=[pl.BlockSpec(memory_space=pl.ANY)],
        out_specs=[pl.BlockSpec(memory_space=pl.ANY)] * 2,
        out_shape=out_shape,
        scratch_shapes=[pltpu.VMEM((pairs, tiles, TILE, HEAD), BF)]
        + [pltpu.VMEM(out.shape, BF) for out in out_shape]
        + [pltpu.VMEM((blocks, BLK, HEAD), F32)] * 2
        + [
            pltpu.VMEM((pairs, META, HEAD), BF),
            pltpu.VMEM((pairs, HEAD), jnp.int32),
            pltpu.SMEM((pairs, HEAD), jnp.int32),
            pltpu.SMEM((LIST,), jnp.int32),
            pltpu.SMEM((blocks,), jnp.int32),
            pltpu.SemaphoreType.DMA((8,)),
        ]
        + [pltpu.VMEM(wide, F32)] * 4
        + [pltpu.VMEM(wide, BF)] * 4,
        compiler_params=pltpu.CompilerParams(vmem_limit_bytes=VMEM_ALL),
        cost_estimate=pl.CostEstimate(
            flops=20 * blocks * slots * BLK * BLK * HEAD,
            bytes_accessed=2 * states.size + 6 * blocks * BLK * HEAD,
            transcendentals=blocks * slots * BLK * BLK,
        ),
        name="attention",
    )(states.reshape(pairs, tiles, TILE, HEAD))
    return grads.reshape(pairs, 2 * rows, HEAD), dq.reshape(pairs, rows, HEAD)


def down_kernel(grads_ref, up_ref, x_ref, out_ref):
    heads = grads_ref.shape[0]
    rows = x_ref.shape[0]
    low = []
    for t in range(2):
        part = slice(t * rows, (t + 1) * rows)
        full = jnp.concatenate([grads_ref[h, part, :] for h in range(heads)], axis=1)
        low.append(dot(full, up_ref[t], NT))
    back_low = jnp.concatenate(low, axis=1).astype(BF)
    terms = dot(back_low, x_ref[...], TN).astype(BF)
    for h in range(heads):
        out_ref[h] = terms[:, h * HEAD:(h + 1) * HEAD]


def down_terms(grads, adapter_up, x):
    heads = grads.shape[0]
    rows, feats = x.shape
    return pl.pallas_call(
        down_kernel,
        in_specs=[pl.BlockSpec(memory_space=pltpu.VMEM)] * 3,
        out_specs=pl.BlockSpec(memory_space=pltpu.VMEM),
        out_shape=jax.ShapeDtypeStruct((heads, 2 * adapter_up.shape[1], HEAD), BF),
        compiler_params=pltpu.CompilerParams(vmem_limit_bytes=VMEM_ALL),
        cost_estimate=pl.CostEstimate(
            flops=8 * rows * feats * adapter_up.shape[1],
            bytes_accessed=12 * rows * feats,
            transcendentals=0,
        ),
        name="down_terms",
    )(grads, adapter_up, x)


def unpack(grads, rows):
    parts = grads.reshape(grads.shape[0], -1, rows, HEAD)
    return [parts[:, t].transpose(1, 0, 2).reshape(rows, -1) for t in range(parts.shape[1])]


def swap(x, axis):
    return lax.all_to_all(x, axis, split_axis=0, concat_axis=0, tiled=True)


def sum_windows(x):
    n = lax.axis_size("dp")
    if n % 8 or n > 8:
        step = 1
        while step < n:
            x = x + lax.ppermute(x, "dp", [(i, i ^ step) for i in range(n)])
            step *= 2
        return x
    near = [lax.ppermute(x, "dp", [(i, i ^ step) for i in range(n)]) for step in (1, 2, 3)]
    x = (x + near[0]) + (near[1] + near[2])
    return x + lax.ppermute(x, "dp", [(i, (i + (2 if i % 4 >= 2 else -2)) % n) for i in range(n)])


def shards(
    features,
    query_states,
    key_states,
    value_states,
    cotangent,
    adapter_down,
    adapter_up,
    block_lists,
    block_counts,
):
    zones = lax.axis_size("zone")
    windows = lax.axis_size("dp")
    rows = query_states.shape[1]
    rank = adapter_down.shape[1]
    all_rows = zones * rows
    x = features[0]

    sent = pack(
        block_lists[0], block_counts, query_states[0], key_states[0], value_states[0], cotangent[0]
    )
    states = swap(sent, "zone")

    low = lowrank(x, adapter_down.reshape(2 * rank, -1), zones)
    low, states = lax.optimization_barrier((low, states))
    low_all = swap(low, "zone")

    grads, dq = attention(states, rows, block_lists.shape[2] + 1)
    grads, low_all = lax.optimization_barrier((grads, low_all))
    home = swap(grads, "zone")

    stacked = grads.reshape(zones, 2, rows, HEAD)
    up = jnp.concatenate(
        [
            jnp.einsum(
                "zra,zrf->af",
                low_all[:, :, t * rank:(t + 1) * rank],
                stacked[:, t],
                preferred_element_type=F32,
            )
            for t in range(2)
        ]
    )
    up = sum_windows(up)

    terms, up = lax.optimization_barrier((down_terms(home, adapter_up, x), up))
    terms = swap(terms, "zone")
    key_grad, value_grad = unpack(home, rows)
    dq, terms, key_grad, value_grad = lax.optimization_barrier((dq, terms, key_grad, value_grad))
    dq = swap(dq, "zone")
    down = sum_windows(jnp.sum(terms.astype(F32), axis=0))
    (query_grad,) = unpack(dq, rows)
    factor = 1.0 / math.sqrt(windows * all_rows)
    return (
        query_grad[None],
        key_grad[None],
        value_grad[None],
        down.reshape(2, rank, HEAD) * factor,
        up.reshape(2, rank, HEAD) * factor,
    )


def solution(mesh):
    rows = P("dp", "zone", None)
    cols = P(None, None, "zone")
    in_specs = (rows, rows, rows, rows, rows, P(), P(), rows, P("dp", "zone"))
    out_specs = (rows, rows, rows, cols, cols)
    return jax.shard_map(shards, mesh=mesh, in_specs=in_specs, out_specs=out_specs, check_vma=False)
```

time: 186 us -> 177 us (0.952)
  Pallas kernels: 32.2 us -> 27.4 us
  starting transfers between devices: 62.3 us -> 57.6 us
    ppermute x6 -> x8, starting transfers between devices: 24.9 us -> 20.1 us  [the longest x6 10.7 us: sum_windows(): lax.ppermute(x, 'dp', [(i, i ^ step) for i in range(n)])]
    pallas_call x1, Pallas kernels: 20.8 us -> 16.1 us  [attention(): pl.pallas_call(functools.partial(attention_kernel, slots=slots), in_specs...]
    all_to_all x5, waiting for transfers between devices: 65 us -> 63.1 us  [swap(): return lax.all_to_all(x, axis, split_axis=0, concat_axis=0, tiled=True)]
    ppermute x6 -> x8, waiting for transfers between devices: 14.4 us -> 16.2 us  [the longest x6 11.2 us: sum_windows(): lax.ppermute(x, 'dp', [(i, i ^ step) for i in range(n)])]
  transfers between devices with their start and end apart: 11 -> 13, of which waited for: 9 -> 10; matrix products, arithmetic and copies ran while one was open for 4% -> 5% of each run, Pallas kernels for 13% -> 11%
where the time goes in v3:
time: 177 us; the launch traced here: 175 us
  waiting for transfers between devices  79.3 us (45%)
  starting transfers between devices  57.6 us (33%)
  Pallas kernels  27.4 us (15%)
  local copies, waits for them, and re-layouts  5.28 us (3%)
  matrix products  3.62 us (2%)
    all_to_all x5, waiting for transfers between devices, swap(): return lax.all_to_all(x, axis, split_axis=0, concat_axis=0, tiled=True)  63.1 us
    all_to_all x5, starting transfers between devices, swap(): return lax.all_to_all(x, axis, split_axis=0, concat_axis=0, tiled=True)  37.5 us
    pallas_call x1, Pallas kernels, attention(): pl.pallas_call(functools.partial(attention_kernel, slots=slots), in_specs...  16.1 us
    ppermute x6, waiting for transfers between devices, sum_windows(): lax.ppermute(x, 'dp', [(i, i ^ step) for i in range(n)])  11.2 us
    ppermute x6, starting transfers between devices, sum_windows(): lax.ppermute(x, 'dp', [(i, i ^ step) for i in range(n)])  10.7 us
    ppermute x2, starting transfers between devices, sum_windows(): lax.ppermute(x, 'dp', [(i, (i + (2 if i % 4 >= 2 else -2)) % n) for i in...  9.4 us
    ppermute x2, waiting for transfers between devices, sum_windows(): lax.ppermute(x, 'dp', [(i, (i + (2 if i % 4 >= 2 else -2)) % n) for i in...  4.94 us
    pallas_call x1, Pallas kernels, down_terms(): pl.pallas_call(down_kernel, in_specs=[pl.BlockSpec(memory_space=pltpu.VME...  4.34 us
  transfers between devices with their start and end apart: 13, of which 10 were waited for; matrix products, arithmetic and copies ran while one was open for 5% of the time, Pallas kernels for 11%

profile of v3, /device:TPU:2, one launch (start us, length us, event | category | flops | bytes accessed | tf_op | source)
XLA Modules:
  0.0 175.5 jit_solution(13045034582969275117)
XLA Ops:
  0.6 4.0 %pack.1 = bf16[32,528,128]{2,1,0:T(8,128)(2,1)} custom-call(s32[2,8]{1,0:T(2,128)} %bitcast.58, s32[1,2]{1,0:T(1,128)} %counts_ref.1, bf16[128,4096]{1,0:T(8,128)(2,1)} %bitcast.49, bf16[128,4096]{1,0:T(8,128)(2,1)} %bitcast.50, bf16[128,4096]{1,0:T(8,128)(2,1)} %bitcast.51, bf16[128,4096]{1,0:T(8,128)(2,1)} %bitcast.52), custom_call_target="tpu_custom_call" | custom-call | bytes 8388608 | tf_op jit(solution)/shard_map/pack/pallas_call | solution.py:55
  4.6 7.7 %all-to-all-start = ((bf16[32,528,128]{2,1,0:T(8,128)(2,1)}), bf16[32,528,128]{2,1,0:T(8,128)(2,1)}, u32[]{:S(2)}, u32[]{:S(2)}) async-start(bf16[32,528,128]{2,1,0:T(8,128)(2,1)} %pack.1), calls=%async_computation | async-start | bytes 8650752 | tf_op jit(solution)/shard_map/all_to_all | solution.py:367
  12.3 3.0 %lowrank.1 = bf16[32,128,128]{2,1,0:T(8,128)(2,1)} custom-call(bf16[128,4096]{1,0:T(8,128)(2,1)} %bitcast.45, bf16[128,4096]{1,0:T(8,128)(2,1)} %bitcast.53), custom_call_target="tpu_custom_call" | custom-call | flops 134217728 | bytes 3145728 | tf_op jit(solution)/shard_map/lowrank/pallas_call | solution.py:75
  15.3 49.0 %all-to-all-done = bf16[32,528,128]{2,1,0:T(8,128)(2,1)} async-done(((bf16[32,528,128]{2,1,0:T(8,128)(2,1)}), bf16[32,528,128]{2,1,0:T(8,128)(2,1)}, u32[]{:S(2)}, u32[]{:S(2)}) %all-to-all-start) | async-done | bytes 4325408 | tf_op jit(solution)/shard_map/all_to_all | solution.py:367
  64.3 9.0 %all-to-all-start.1 = ((bf16[32,128,128]{2,1,0:T(8,128)(2,1)}), bf16[32,128,128]{2,1,0:T(8,128)(2,1)}, u32[]{:S(2)}, u32[]{:S(2)}) async-start(bf16[32,128,128]{2,1,0:T(8,128)(2,1)} %lowrank.1), calls=%async_computation.1 | async-start | bytes 2097152 | tf_op jit(solution)/shard_map/all_to_all | solution.py:367
  73.4 16.1 %attention.1 = (bf16[32,2,128,128]{3,2,1,0:T(8,128)(2,1)}, bf16[64,64,128]{2,1,0:T(8,128)(2,1)}) custom-call(bf16[32,33,16,128]{3,2,1,0:T(8,128)(2,1)} %bitcast.7.states_hbm), custom_call_target="tpu_custom_call" | custom-call | flops 6039797760 | bytes 7471104 | tf_op jit(solution)/shard_map/attention/pallas_call | solution.py:300
  89.4 7.6 %all-to-all-start.2 = ((bf16[32,256,128]{2,1,0:T(8,128)(2,1)}), bf16[32,256,128]{2,1,0:T(8,128)(2,1)}, u32[]{:S(2)}, u32[]{:S(2)}) async-start(bf16[32,256,128]{2,1,0:T(8,128)(2,1)} %bitcast.48), calls=%async_computation.2 | async-start | bytes 4194304 | tf_op jit(solution)/shard_map/all_to_all | solution.py:367
  97.0 1.7 convolution_bitcast_fusion.1
  98.7 2.0 %convolution_bitcast_fusion = f32[64,128]{1,0:T(8,128)S(1)} fusion(bf16[32,2,128,128]{3,2,1,0:T(8,128)(2,1)S(1)} %copy-done, bf16[32,128,128]{2,1,0:T(8,128)(2,1)} %all-to-all-done.1), kind=kOutput, calls=%fused_computation.1 | convolution fusion | flops 67108864 | bytes 2129920 | tf_op jit(solution)/shard_map/zra,zrf->af/dot_general | solution.py:417
  100.7 4.4 %collective-permute-start.1 = (f32[128,128]{1,0:T(8,128)S(1)}, f32[128,128]{1,0:T(8,128)S(1)}, u32[]{:S(2)}, u32[]{:S(2)}) collective-permute-start(f32[128,128]{1,0:T(8,128)S(1)} %pad_maximum_fusion), channel_id=1, source_target_pairs={{0,64},{32,96},{64,0},{96,32},{128,192},{160,224},{192,128},{224,1... | collective-permute-start | bytes 196616 | tf_op jit(solution)/shard_map/ppermute | solution.py:378
  105.1 1.0 collective-permute-start.2
  106.1 3.3 %collective-permute-done.1 = f32[128,128]{1,0:T(8,128)S(1)} collective-permute-done((f32[128,128]{1,0:T(8,128)S(1)}, f32[128,128]{1,0:T(8,128)S(1)}, u32[]{:S(2)}, u32[]{:S(2)}) %collective-permute-start.1) | collective-permute-done | bytes 65568 | tf_op jit(solution)/shard_map/ppermute | solution.py:378
  109.4 2.1 %collective-permute-done.2 = f32[128,128]{1,0:T(8,128)S(1)} collective-permute-done((f32[128,128]{1,0:T(8,128)S(1)}, f32[128,128]{1,0:T(8,128)S(1)}, u32[]{:S(2)}, u32[]{:S(2)}) %collective-permute-start.2) | collective-permute-done | bytes 65568 | tf_op jit(solution)/shard_map/ppermute | solution.py:378
  111.6 5.3 %collective-permute-start.3 = (f32[128,128]{1,0:T(8,128)S(1)}, f32[128,128]{1,0:T(8,128)S(1)}, u32[]{:S(2)}, u32[]{:S(2)}) collective-permute-start(f32[128,128]{1,0:T(8,128)S(1)} %add_add_fusion.1), channel_id=1, source_target_pairs={{0,192},{32,224},{64,128},{96,160},{128,64},{160,96},{192,0},{224,... | collective-permute-start | bytes 196616 | tf_op jit(solution)/shard_map/ppermute | solution.py:380
  116.9 3.1 %collective-permute-done.3 = f32[128,128]{1,0:T(8,128)S(1)} collective-permute-done((f32[128,128]{1,0:T(8,128)S(1)}, f32[128,128]{1,0:T(8,128)S(1)}, u32[]{:S(2)}, u32[]{:S(2)}) %collective-permute-start.3) | collective-permute-done | bytes 65568 | tf_op jit(solution)/shard_map/ppermute | solution.py:380
  120.1 3.0 %all-to-all-done.2.grads_ref = bf16[32,256,128]{2,1,0:T(8,128)(2,1)} async-done(((bf16[32,256,128]{2,1,0:T(8,128)(2,1)}), bf16[32,256,128]{2,1,0:T(8,128)(2,1)}, u32[]{:S(2)}, u32[]{:S(2)}) %all-to-all-start.2) | async-done | bytes 2097184 | tf_op jit(solution)/shard_map/all_to_all | solution.py:367
  123.0 4.3 %down_terms.1 = bf16[32,128,128]{2,1,0:T(8,128)(2,1)} custom-call(bf16[32,256,128]{2,1,0:T(8,128)(2,1)} %all-to-all-done.2.grads_ref, bf16[2,64,4096]{2,1,0:T(8,128)(2,1)} %up_ref.1, bf16[128,4096]{1,0:T(8,128)(2,1)} %bitcast.46), custom_call_target="tpu_custom_call" | custom-call | flops 268435456 | bytes 6291456 | tf_op jit(solution)/shard_map/down_terms/pallas_call | solution.py:346
  127.4 6.8 %all-to-all-start.3 = ((bf16[32,128,128]{2,1,0:T(8,128)(2,1)}), bf16[32,128,128]{2,1,0:T(8,128)(2,1)S(1)}, u32[]{:S(2)}, u32[]{:S(2)}) async-start(bf16[32,128,128]{2,1,0:T(8,128)(2,1)} %down_terms.1), calls=%async_computation.3 | async-start | bytes 2097152 | tf_op jit(solution)/shard_map/all_to_all | solution.py:367
  134.2 1.7 slice_bitcast_fusion
  135.9 1.6 copy_bitcast_fusion
  137.5 11.2 %all-to-all-done.3 = bf16[32,128,128]{2,1,0:T(8,128)(2,1)S(1)} async-done(((bf16[32,128,128]{2,1,0:T(8,128)(2,1)}), bf16[32,128,128]{2,1,0:T(8,128)(2,1)S(1)}, u32[]{:S(2)}, u32[]{:S(2)}) %all-to-all-start.3) | async-done | bytes 1048608 | tf_op jit(solution)/shard_map/all_to_all | solution.py:367
  148.7 6.4 %all-to-all-start.4 = ((bf16[32,128,128]{2,1,0:T(8,128)(2,1)}), bf16[32,128,128]{2,1,0:T(8,128)(2,1)S(1)}, u32[]{:S(2)}, u32[]{:S(2)}) async-start(bf16[32,128,128]{2,1,0:T(8,128)(2,1)} %bitcast.8), calls=%async_computation.4 | async-start | bytes 2097152 | tf_op jit(solution)/shard_map/all_to_all | solution.py:367
  155.3 4.6 %collective-permute-start.6 = (f32[128,128]{1,0:T(8,128)S(1)}, f32[128,128]{1,0:T(8,128)S(1)}, u32[]{:S(2)}, u32[]{:S(2)}) collective-permute-start(f32[128,128]{1,0:T(8,128)S(1)} %convert_reduce_fusion), channel_id=1, source_target_pairs={{0,96},{32,64},{64,32},{96,0},{128,224},{160,192},{192,160},{224,1... | collective-permute-start | bytes 196616 | tf_op jit(solution)/shard_map/ppermute | solution.py:378
  159.9 0.7 collective-permute-start.4
  160.5 1.8 %collective-permute-done.6 = f32[128,128]{1,0:T(8,128)S(1)} collective-permute-done((f32[128,128]{1,0:T(8,128)S(1)}, f32[128,128]{1,0:T(8,128)S(1)}, u32[]{:S(2)}, u32[]{:S(2)}) %collective-permute-start.6) | collective-permute-done | bytes 65568 | tf_op jit(solution)/shard_map/ppermute | solution.py:378
  162.4 3.9 %collective-permute-done.5 = f32[128,128]{1,0:T(8,128)S(1)} collective-permute-done((f32[128,128]{1,0:T(8,128)S(1)}, f32[128,128]{1,0:T(8,128)S(1)}, u32[]{:S(2)}, u32[]{:S(2)}) %collective-permute-start.5) | collective-permute-done | bytes 65568 | tf_op jit(solution)/shard_map/ppermute | solution.py:378
  166.3 4.1 %collective-permute-start.7 = (f32[128,128]{1,0:T(8,128)S(1)}, f32[128,128]{1,0:T(8,128)S(1)}, u32[]{:S(2)}, u32[]{:S(2)}) collective-permute-start(f32[128,128]{1,0:T(8,128)S(1)} %add_add_fusion), channel_id=1, source_target_pairs={{0,192},{32,224},{64,128},{96,160},{128,64},{160,96},{192,0},{224,... | collective-permute-start | bytes 196616 | tf_op jit(solution)/shard_map/ppermute | solution.py:380
  170.4 0.6 broadcast_multiply_fusion
  171.0 1.8 %collective-permute-done.7 = f32[128,128]{1,0:T(8,128)S(1)} collective-permute-done((f32[128,128]{1,0:T(8,128)S(1)}, f32[128,128]{1,0:T(8,128)S(1)}, u32[]{:S(2)}, u32[]{:S(2)}) %collective-permute-start.7) | collective-permute-done | bytes 65568 | tf_op jit(solution)/shard_map/ppermute | solution.py:380
  172.8 0.6 add_multiply_fusion
  173.5 0.7 copy.20
  174.2 1.3 broadcast_in_dim_reshape.3
  (13 shorter events, 0.4 us)
Async XLA Ops:
  4.6 59.7 %all-to-all-start = ((bf16[32,528,128]{2,1,0:T(8,128)(2,1)}), bf16[32,528,128]{2,1,0:T(8,128)(2,1)}, u32[]{:S(2)}, u32[]{:S(2)}) async-start(bf16[32,528,128]{2,1,0:T(8,128)(2,1)} %pack.1), calls=%async_computation | async-start | bytes 8650752 | tf_op jit(solution)/shard_map/all_to_all | solution.py:367
  64.3 25.1 %all-to-all-start.1 = ((bf16[32,128,128]{2,1,0:T(8,128)(2,1)}), bf16[32,128,128]{2,1,0:T(8,128)(2,1)}, u32[]{:S(2)}, u32[]{:S(2)}) async-start(bf16[32,128,128]{2,1,0:T(8,128)(2,1)} %lowrank.1), calls=%async_computation.1 | async-start | bytes 2097152 | tf_op jit(solution)/shard_map/all_to_all | solution.py:367
  89.4 7.6 %copy-start = (bf16[32,2,128,128]{3,2,1,0:T(8,128)(2,1)S(1)}, bf16[32,2,128,128]{3,2,1,0:T(8,128)(2,1)}, u32[]{:S(2)}) copy-start(bf16[32,2,128,128]{3,2,1,0:T(8,128)(2,1)} %get-tuple-element.19) | copy-start | bytes 6291460
  89.4 33.6 %all-to-all-start.2 = ((bf16[32,256,128]{2,1,0:T(8,128)(2,1)}), bf16[32,256,128]{2,1,0:T(8,128)(2,1)}, u32[]{:S(2)}, u32[]{:S(2)}) async-start(bf16[32,256,128]{2,1,0:T(8,128)(2,1)} %bitcast.48), calls=%async_computation.2 | async-start | bytes 4194304 | tf_op jit(solution)/shard_map/all_to_all | solution.py:367
  100.7 8.7 %collective-permute-start.1 = (f32[128,128]{1,0:T(8,128)S(1)}, f32[128,128]{1,0:T(8,128)S(1)}, u32[]{:S(2)}, u32[]{:S(2)}) collective-permute-start(f32[128,128]{1,0:T(8,128)S(1)} %pad_maximum_fusion), channel_id=1, source_target_pairs={{0,64},{32,96},{64,0},{96,32},{128,192},{160,224},{192,128},{224,1... | collective-permute-start | bytes 196616 | tf_op jit(solution)/shard_map/ppermute | solution.py:378
  105.1 6.4 %collective-permute-start.2 = (f32[128,128]{1,0:T(8,128)S(1)}, f32[128,128]{1,0:T(8,128)S(1)}, u32[]{:S(2)}, u32[]{:S(2)}) collective-permute-start(f32[128,128]{1,0:T(8,128)S(1)} %pad_maximum_fusion), channel_id=1, source_target_pairs={{0,96},{32,64},{64,32},{96,0},{128,224},{160,192},{192,160},{224,1... | collective-permute-start | bytes 196616 | tf_op jit(solution)/shard_map/ppermute | solution.py:378
  106.1 5.5 %collective-permute-start = (f32[128,128]{1,0:T(8,128)S(1)}, f32[128,128]{1,0:T(8,128)S(1)}, u32[]{:S(2)}, u32[]{:S(2)}) collective-permute-start(f32[128,128]{1,0:T(8,128)S(1)} %pad_maximum_fusion), channel_id=1, source_target_pairs={{0,32},{32,0},{64,96},{96,64},{128,160},{160,128},{192,224},{224,1... | collective-permute-start | bytes 196616 | tf_op jit(solution)/shard_map/ppermute | solution.py:378
  111.6 8.4 %collective-permute-start.3 = (f32[128,128]{1,0:T(8,128)S(1)}, f32[128,128]{1,0:T(8,128)S(1)}, u32[]{:S(2)}, u32[]{:S(2)}) collective-permute-start(f32[128,128]{1,0:T(8,128)S(1)} %add_add_fusion.1), channel_id=1, source_target_pairs={{0,192},{32,224},{64,128},{96,160},{128,64},{160,96},{192,0},{224,... | collective-permute-start | bytes 196616 | tf_op jit(solution)/shard_map/ppermute | solution.py:380
  127.4 21.4 %all-to-all-start.3 = ((bf16[32,128,128]{2,1,0:T(8,128)(2,1)}), bf16[32,128,128]{2,1,0:T(8,128)(2,1)S(1)}, u32[]{:S(2)}, u32[]{:S(2)}) async-start(bf16[32,128,128]{2,1,0:T(8,128)(2,1)} %down_terms.1), calls=%async_computation.3 | async-start | bytes 2097152 | tf_op jit(solution)/shard_map/all_to_all | solution.py:367
  148.7 24.8 %all-to-all-start.4 = ((bf16[32,128,128]{2,1,0:T(8,128)(2,1)}), bf16[32,128,128]{2,1,0:T(8,128)(2,1)S(1)}, u32[]{:S(2)}, u32[]{:S(2)}) async-start(bf16[32,128,128]{2,1,0:T(8,128)(2,1)} %bitcast.8), calls=%async_computation.4 | async-start | bytes 2097152 | tf_op jit(solution)/shard_map/all_to_all | solution.py:367
  155.3 7.1 %collective-permute-start.6 = (f32[128,128]{1,0:T(8,128)S(1)}, f32[128,128]{1,0:T(8,128)S(1)}, u32[]{:S(2)}, u32[]{:S(2)}) collective-permute-start(f32[128,128]{1,0:T(8,128)S(1)} %convert_reduce_fusion), channel_id=1, source_target_pairs={{0,96},{32,64},{64,32},{96,0},{128,224},{160,192},{192,160},{224,1... | collective-permute-start | bytes 196616 | tf_op jit(solution)/shard_map/ppermute | solution.py:378
  159.9 6.4 %collective-permute-start.5 = (f32[128,128]{1,0:T(8,128)S(1)}, f32[128,128]{1,0:T(8,128)S(1)}, u32[]{:S(2)}, u32[]{:S(2)}) collective-permute-start(f32[128,128]{1,0:T(8,128)S(1)} %convert_reduce_fusion), channel_id=1, source_target_pairs={{0,64},{32,96},{64,0},{96,32},{128,192},{160,224},{192,128},{224,1... | collective-permute-start | bytes 196616 | tf_op jit(solution)/shard_map/ppermute | solution.py:378
  159.9 6.4 %collective-permute-start.4 = (f32[128,128]{1,0:T(8,128)S(1)}, f32[128,128]{1,0:T(8,128)S(1)}, u32[]{:S(2)}, u32[]{:S(2)}) collective-permute-start(f32[128,128]{1,0:T(8,128)S(1)} %convert_reduce_fusion), channel_id=1, source_target_pairs={{0,32},{32,0},{64,96},{96,64},{128,160},{160,128},{192,224},{224,1... | collective-permute-start | bytes 196616 | tf_op jit(solution)/shard_map/ppermute | solution.py:378
  166.3 6.6 %collective-permute-start.7 = (f32[128,128]{1,0:T(8,128)S(1)}, f32[128,128]{1,0:T(8,128)S(1)}, u32[]{:S(2)}, u32[]{:S(2)}) collective-permute-start(f32[128,128]{1,0:T(8,128)S(1)} %add_add_fusion), channel_id=1, source_target_pairs={{0,192},{32,224},{64,128},{96,160},{128,64},{160,96},{192,0},{224,... | collective-permute-start | bytes 196616 | tf_op jit(solution)/shard_map/ppermute | solution.py:380

commit v4 on v3

--- a/solution.py
+++ b/solution.py
@@ -11,9 +11,12 @@
 HEAD = 128
 BLK = 64
 VMEM_ALL = 63 << 20
+VMEM_SOME = 12 << 20
 TILE = 16
 LIST = 16
 META = 16
+CHUNKS = 4
+PACK_CHUNKS = 2
 BF = jnp.bfloat16
 F32 = jnp.float32
 NT = (((1,), (1,)), ((), ()))
@@ -29,8 +32,28 @@
     return pl.BlockSpec(memory_space=space)
 
 
-def pack_kernel(lists_ref, counts_ref, q_ref, k_ref, v_ref, g_ref, out_ref):
-    rows = q_ref.shape[0]
+def pack_kernel(lists_ref, counts_ref, *refs):
+    ins, (x_hbm, down_hbm, out_hbm), refs = refs[:4], refs[4:7], refs[7:]
+    bufs, (x_ref, down_ref, out_ref, sems) = refs[:4], refs[4:]
+    rows, feats = bufs[0].shape
+    heads = feats // HEAD
+    chunk = feats // PACK_CHUNKS
+    states_rows = 4 * rows + META
+    reads = []
+    for i in range(PACK_CHUNKS):
+        at = (slice(None), pl.ds(i * chunk, chunk))
+        for t in range(4):
+            reads.append(
+                pltpu.make_async_copy(ins[t].at[at], bufs[t].at[at], sems.at[i * 4 + t])
+            )
+            reads[-1].start()
+    last = 5 * PACK_CHUNKS
+    others = [
+        pltpu.make_async_copy(x_hbm, x_ref, sems.at[last]),
+        pltpu.make_async_copy(down_hbm, down_ref, sems.at[last + 1]),
+    ]
+    for read in others:
+        read.start()
     blocks, nbr = lists_ref.shape
     row = lax.broadcasted_iota(jnp.int32, (META, HEAD), 0)
     lane = lax.broadcasted_iota(jnp.int32, (META, HEAD), 1)
@@ -40,49 +63,88 @@
             value = lists_ref[b, n - 1] if n else counts_ref[0, b]
             meta = jnp.where((row == 0) & (lane == b * LIST + n), value, meta)
     meta = meta.astype(F32).astype(BF)
-    for j in range(out_ref.shape[0]):
-        cols = slice(j * HEAD, (j + 1) * HEAD)
-        for t, ref in enumerate((q_ref, k_ref, v_ref, g_ref)):
-            out_ref[j, t * rows:(t + 1) * rows, :] = ref[:, cols]
-        out_ref[j, 4 * rows:, :] = meta
-
-
-def pack(lists, counts, q, k, v, g, heads_per_step=16):
+    writes = []
+    for i in range(PACK_CHUNKS):
+        for t in range(4):
+            reads[i * 4 + t].wait()
+        here = heads // PACK_CHUNKS
+        for j in range(i * here, (i + 1) * here):
+            cols = slice(j * HEAD, (j + 1) * HEAD)
+            for t in range(4):
+                out_ref[j, t * rows:(t + 1) * rows, :] = bufs[t][:, cols]
+            out_ref[j, 4 * rows:states_rows, :] = meta
+        at = (pl.ds(i * here, here), pl.ds(0, states_rows))
+        writes.append(pltpu.make_async_copy(out_ref.at[at], out_hbm.at[at], sems.at[4 * PACK_CHUNKS + i]))
+        writes[-1].start()
+    for read in others:
+        read.wait()
+    low = dot(x_ref[...], down_ref[...], NT).astype(BF)
+    half, rank = rows // 2, low.shape[1] // 2
+    for t in range(2):
+        part = low[:, t * rank:(t + 1) * rank]
+        part = jnp.concatenate([part[:half], part[half:]], axis=1)
+        for j in range(t, heads, 2):
+            out_ref[j, states_rows:, :] = part
+    at = (slice(None), pl.ds(states_rows, half))
+    writes.append(pltpu.make_async_copy(out_ref.at[at], out_hbm.at[at], sems.at[last]))
+    writes[-1].start()
+    for write in writes:
+        write.wait()
+
+
+def pack(lists, counts, q, k, v, g, x, down):
     rows, feats = q.shape
-    heads = feats // HEAD
-    out_rows = 4 * rows + META
-    spec = pl.BlockSpec((rows, heads_per_step * HEAD), lambda i: (0, i))
+    out = (feats // HEAD, 4 * rows + META + rows // 2, HEAD)
     return pl.pallas_call(
         pack_kernel,
-        grid=(heads // heads_per_step,),
-        in_specs=[pl.BlockSpec(memory_space=pltpu.SMEM)] * 2 + [spec] * 4,
-        out_specs=pl.BlockSpec((heads_per_step, out_rows, HEAD), lambda i: (i, 0, 0)),
-        out_shape=jax.ShapeDtypeStruct((heads, out_rows, HEAD), BF),
+        in_specs=[pl.BlockSpec(memory_space=pltpu.SMEM)] * 2
+        + [pl.BlockSpec(memory_space=pl.ANY)] * 6,
+        out_specs=pl.BlockSpec(memory_space=pl.ANY),
+        out_shape=jax.ShapeDtypeStruct(out, BF),
+        scratch_shapes=[pltpu.VMEM((rows, feats), BF)] * 5
+        + [
+            pltpu.VMEM(down.shape, BF),
+            pltpu.VMEM(out, BF),
+            pltpu.SemaphoreType.DMA((5 * PACK_CHUNKS + 2,)),
+        ],
         compiler_params=pltpu.CompilerParams(vmem_limit_bytes=VMEM_ALL),
         cost_estimate=pl.CostEstimate(flops=0, bytes_accessed=16 * rows * feats, transcendentals=0),
         name="pack",
-    )(lists, counts, q, k, v, g)
-
-
-def lowrank_kernel(x_ref, down_ref, out_ref):
-    low = dot(x_ref[...], down_ref[...], NT).astype(BF)
-    for j in range(out_ref.shape[0]):
-        out_ref[j] = low
-
-
-def lowrank(x, down, copies):
-    rows, feats = x.shape
+    )(lists, counts, q, k, v, g, x, down)
+
+
+def up_kernel(parity_ref, own_ref, other_ref, grads_ref, out_ref):
+    parts, half, lanes = own_ref.shape
+    rank = lanes // 2
+    mine, other = own_ref[...], other_ref[...]
+    for t in range(2):
+        low = jnp.where(parity_ref[0] == t, mine, other).reshape(parts * half, lanes)
+        first = 2 * t * half
+        grads = jnp.concatenate(
+            [
+                grads_ref[:, first:first + half, :].reshape(parts * half, HEAD),
+                grads_ref[:, first + half:first + 2 * half, :].reshape(parts * half, HEAD),
+            ],
+            axis=1,
+        )
+        both = dot(low, grads, TN)
+        out_ref[t * rank:(t + 1) * rank, :] = both[:rank, :HEAD] + both[rank:, HEAD:]
+
+
+def up_terms(parity, own, other, grads):
+    lanes = own.shape[2]
     return pl.pallas_call(
-        lowrank_kernel,
-        in_specs=[pl.BlockSpec(memory_space=pltpu.VMEM)] * 2,
+        up_kernel,
+        in_specs=[pl.BlockSpec(memory_space=pltpu.SMEM)]
+        + [pl.BlockSpec(memory_space=pltpu.VMEM)] * 3,
         out_specs=pl.BlockSpec(memory_space=pltpu.VMEM),
-        out_shape=jax.ShapeDtypeStruct((copies, rows, down.shape[0]), BF),
-        compiler_params=pltpu.CompilerParams(vmem_limit_bytes=VMEM_ALL),
+        out_shape=jax.ShapeDtypeStruct((lanes, HEAD), F32),
+        compiler_params=pltpu.CompilerParams(vmem_limit_bytes=VMEM_SOME),
         cost_estimate=pl.CostEstimate(
-            flops=2 * rows * feats * down.shape[0], bytes_accessed=6 * rows * feats, transcendentals=0
+            flops=4 * own.size * HEAD * 2, bytes_accessed=4 * own.size + 2 * grads.size, transcendentals=0
         ),
-        name="lowrank",
-    )(x, down)
+        name="up_terms",
+    )(parity, own, other, grads)
 
 
 def blockdiag(x):
@@ -112,7 +174,7 @@
 ):
     blocks = dk_ref.shape[0]
     pairs = blocks // 2
-    stride = states_hbm.shape[1]
+    stride = states_ref.shape[1]
     block_tiles = BLK // TILE
     part_tiles = 2 * block_tiles
     least = 2
@@ -123,10 +185,9 @@
 
     copy_meta = pltpu.make_async_copy(states_hbm.at[:, stride - 1], meta_ref, sems.at[0])
     copy_meta.start()
-    copy_states = pltpu.make_async_copy(states_hbm, states_ref, sems.at[1])
+    copy_states = pltpu.make_async_copy(states_hbm.at[:, pl.ds(0, stride)], states_ref, sems.at[1])
     copy_states.start()
     dk_ref[...] = jnp.zeros_like(dk_ref)
-    dv_ref[...] = jnp.zeros_like(dv_ref)
 
     copy_meta.wait()
     info = jnp.sum(meta_ref[...].astype(F32), axis=1).astype(jnp.int32)
@@ -143,6 +204,7 @@
     codes_ref[...] = codes
     copy_codes = pltpu.make_async_copy(codes_ref, ids_ref, sems.at[2])
     copy_codes.start()
+    dv_ref[...] = jnp.zeros_like(dv_ref)
     copy_codes.wait()
 
     def count_of(b):
@@ -265,25 +327,24 @@
         lax.fori_loop(first, until, body, 0)
         first = until
 
-    copy_dq = pltpu.make_async_copy(dq_ref, dq_hbm, sems.at[3])
-    copy_dq.start()
-    chunk = blocks // 4
+    chunk = blocks // CHUNKS
     copies = []
     for start in range(0, blocks, chunk):
 
         def finish(b, carry):
-            half = pl.ds(pl.multiple_of((b & 1) * BLK, BLK), BLK)
-            out_ref[b >> 1, 0, half, :] = (dk_ref[b] * scale).astype(BF)
-            out_ref[b >> 1, 1, half, :] = dv_ref[b].astype(BF)
+            first = pl.multiple_of((b & 1) * BLK, BLK)
+            out_ref[b >> 1, pl.ds(first, BLK), :] = (dk_ref[b] * scale).astype(BF)
+            out_ref[b >> 1, pl.ds(2 * BLK + first, BLK), :] = dv_ref[b].astype(BF)
             return carry
 
         lax.fori_loop(start, start + chunk, finish, 0, unroll=4)
         at = pl.ds(start // 2, chunk // 2)
         copies.append(
-            pltpu.make_async_copy(out_ref.at[at], out_hbm.at[at], sems.at[4 + start // chunk])
+            pltpu.make_async_copy(out_ref.at[at], out_hbm.at[at], sems.at[3 + start // chunk])
         )
         copies[-1].start()
-    copy_dq.wait()
+    copies.append(pltpu.make_async_copy(dq_ref, dq_hbm, sems.at[3 + CHUNKS]))
+    copies[-1].start()
     for copy in copies:
         copy.wait()
 
@@ -291,10 +352,10 @@
 def attention(states, rows, slots):
     pairs = states.shape[0]
     blocks = pairs * rows // BLK
-    tiles = states.shape[1] // TILE
+    tiles = (4 * rows + META) // TILE
     wide = (slots * BLK, 2 * BLK)
     out_shape = [
-        jax.ShapeDtypeStruct((pairs, 2, rows, HEAD), BF),
+        jax.ShapeDtypeStruct((pairs, 2 * rows, HEAD), BF),
         jax.ShapeDtypeStruct((blocks, BLK, HEAD), BF),
     ]
     grads, dq = pl.pallas_call(
@@ -311,7 +372,7 @@
             pltpu.SMEM((pairs, HEAD), jnp.int32),
             pltpu.SMEM((LIST,), jnp.int32),
             pltpu.SMEM((blocks,), jnp.int32),
-            pltpu.SemaphoreType.DMA((8,)),
+            pltpu.SemaphoreType.DMA((4 + CHUNKS,)),
         ]
         + [pltpu.VMEM(wide, F32)] * 4
         + [pltpu.VMEM(wide, BF)] * 4,
@@ -322,8 +383,8 @@
             transcendentals=blocks * slots * BLK * BLK,
         ),
         name="attention",
-    )(states.reshape(pairs, tiles, TILE, HEAD))
-    return grads.reshape(pairs, 2 * rows, HEAD), dq.reshape(pairs, rows, HEAD)
+    )(states.reshape(pairs, -1, TILE, HEAD))
+    return grads, dq.reshape(pairs, rows, HEAD)
 
 
 def down_kernel(grads_ref, up_ref, x_ref, out_ref):
@@ -341,14 +402,13 @@
 
 
 def down_terms(grads, adapter_up, x):
-    heads = grads.shape[0]
     rows, feats = x.shape
     return pl.pallas_call(
         down_kernel,
         in_specs=[pl.BlockSpec(memory_space=pltpu.VMEM)] * 3,
         out_specs=pl.BlockSpec(memory_space=pltpu.VMEM),
-        out_shape=jax.ShapeDtypeStruct((heads, 2 * adapter_up.shape[1], HEAD), BF),
-        compiler_params=pltpu.CompilerParams(vmem_limit_bytes=VMEM_ALL),
+        out_shape=jax.ShapeDtypeStruct((grads.shape[0], 2 * adapter_up.shape[1], HEAD), BF),
+        compiler_params=pltpu.CompilerParams(vmem_limit_bytes=VMEM_SOME),
         cost_estimate=pl.CostEstimate(
             flops=8 * rows * feats * adapter_up.shape[1],
             bytes_accessed=12 * rows * feats,
@@ -358,16 +418,61 @@
     )(grads, adapter_up, x)
 
 
-def unpack(grads, rows):
-    parts = grads.reshape(grads.shape[0], -1, rows, HEAD)
-    return [parts[:, t].transpose(1, 0, 2).reshape(rows, -1) for t in range(parts.shape[1])]
+def unpack_kernel(grads_hbm, *refs):
+    parts = (len(refs) - 2) // 2
+    outs, bufs, grads_ref, sems = refs[:parts], refs[parts:2 * parts], refs[-2], refs[-1]
+    heads, all_rows, _ = grads_ref.shape
+    rows = all_rows // parts
+    here = heads // CHUNKS
+    reads = []
+    for i in range(CHUNKS):
+        at = pl.ds(i * here, here)
+        reads.append(
+            pltpu.make_async_copy(
+                grads_hbm.at[at, pl.ds(0, all_rows)], grads_ref.at[at], sems.at[i]
+            )
+        )
+        reads[-1].start()
+    writes = []
+    for i in range(CHUNKS):
+        reads[i].wait()
+        for t in range(parts):
+            for h in range(i * here, (i + 1) * here):
+                bufs[t][:, h * HEAD:(h + 1) * HEAD] = grads_ref[h, t * rows:(t + 1) * rows, :]
+            at = (slice(None), pl.ds(i * here * HEAD, here * HEAD))
+            sem = sems.at[CHUNKS + i * parts + t]
+            writes.append(pltpu.make_async_copy(bufs[t].at[at], outs[t].at[at], sem))
+            writes[-1].start()
+    for write in writes:
+        write.wait()
+
+
+def unpack(grads, rows, parts):
+    heads = grads.shape[0]
+    out = (rows, heads * HEAD)
+    return pl.pallas_call(
+        unpack_kernel,
+        in_specs=[pl.BlockSpec(memory_space=pl.ANY)],
+        out_specs=[pl.BlockSpec(memory_space=pl.ANY)] * parts,
+        out_shape=[jax.ShapeDtypeStruct(out, BF)] * parts,
+        scratch_shapes=[pltpu.VMEM(out, BF)] * parts
+        + [
+            pltpu.VMEM((heads, parts * rows, HEAD), BF),
+            pltpu.SemaphoreType.DMA((CHUNKS * (1 + parts),)),
+        ],
+        compiler_params=pltpu.CompilerParams(vmem_limit_bytes=VMEM_SOME),
+        cost_estimate=pl.CostEstimate(
+            flops=0, bytes_accessed=4 * parts * rows * heads * HEAD, transcendentals=0
+        ),
+        name="unpack",
+    )(grads)
 
 
 def swap(x, axis):
     return lax.all_to_all(x, axis, split_axis=0, concat_axis=0, tiled=True)
 
 
-def sum_windows(x):
+def sum_windows(x, first=F32):
     n = lax.axis_size("dp")
     if n % 8 or n > 8:
         step = 1
@@ -375,7 +480,12 @@
             x = x + lax.ppermute(x, "dp", [(i, i ^ step) for i in range(n)])
             step *= 2
         return x
-    near = [lax.ppermute(x, "dp", [(i, i ^ step) for i in range(n)]) for step in (1, 2, 3)]
+    if first == BF:
+        x = lax.reduce_precision(x, exponent_bits=8, mantissa_bits=7)
+    near = [
+        lax.ppermute(x.astype(first), "dp", [(i, i ^ step) for i in range(n)]).astype(F32)
+        for step in (1, 2, 3)
+    ]
     x = (x + near[0]) + (near[1] + near[2])
     return x + lax.ppermute(x, "dp", [(i, (i + (2 if i % 4 >= 2 else -2)) % n) for i in range(n)])
 
@@ -398,40 +508,34 @@
     all_rows = zones * rows
     x = features[0]
 
-    sent = pack(
-        block_lists[0], block_counts, query_states[0], key_states[0], value_states[0], cotangent[0]
+    states = swap(
+        pack(
+            block_lists[0],
+            block_counts,
+            query_states[0],
+            key_states[0],
+            value_states[0],
+            cotangent[0],
+            x,
+            adapter_down.reshape(2 * rank, -1),
+        ),
+        "zone",
     )
-    states = swap(sent, "zone")
-
-    low = lowrank(x, adapter_down.reshape(2 * rank, -1), zones)
-    low, states = lax.optimization_barrier((low, states))
-    low_all = swap(low, "zone")
-
     grads, dq = attention(states, rows, block_lists.shape[2] + 1)
-    grads, low_all = lax.optimization_barrier((grads, low_all))
     home = swap(grads, "zone")
 
-    stacked = grads.reshape(zones, 2, rows, HEAD)
-    up = jnp.concatenate(
-        [
-            jnp.einsum(
-                "zra,zrf->af",
-                low_all[:, :, t * rank:(t + 1) * rank],
-                stacked[:, t],
-                preferred_element_type=F32,
-            )
-            for t in range(2)
-        ]
-    )
-    up = sum_windows(up)
+    own = states[:, 4 * rows + META:]
+    other = lax.ppermute(own, "zone", [(i, i ^ 1) for i in range(zones)])
+    parity = (lax.axis_index("zone") & 1).astype(jnp.int32).reshape(1)
+    up = sum_windows(up_terms(parity, own, other, grads))
 
     terms, up = lax.optimization_barrier((down_terms(home, adapter_up, x), up))
     terms = swap(terms, "zone")
-    key_grad, value_grad = unpack(home, rows)
+    key_grad, value_grad = unpack(home, rows, 2)
     dq, terms, key_grad, value_grad = lax.optimization_barrier((dq, terms, key_grad, value_grad))
     dq = swap(dq, "zone")
-    down = sum_windows(jnp.sum(terms.astype(F32), axis=0))
-    (query_grad,) = unpack(dq, rows)
+    down = sum_windows(jnp.sum(terms.astype(F32), axis=0), BF)
+    (query_grad,) = unpack(dq, rows, 1)
     factor = 1.0 / math.sqrt(windows * all_rows)
     return (
         query_grad[None],

time: 177 us -> 170 us (0.960)
  blocking collectives: 0 us -> 63.5 us
  waiting for transfers between devices: 79.3 us -> 31.5 us
  starting transfers between devices: 57.6 us -> 38 us
  matrix products: 3.62 us -> 0 us
    all_to_all x0 -> x1, blocking collectives: none -> 63.5 us  [swap(): return lax.all_to_all(x, axis, split_axis=0, concat_axis=0, tiled=True)]
    all_to_all x5 -> x3, waiting for transfers between devices: 63.1 us -> 12.8 us  [swap(): return lax.all_to_all(x, axis, split_axis=0, concat_axis=0, tiled=True)]
    all_to_all x5 -> x3, starting transfers between devices: 37.5 us -> 19.6 us  [swap(): return lax.all_to_all(x, axis, split_axis=0, concat_axis=0, tiled=True)]
    dot_general x2 -> x0, matrix products: 3.62 us -> none  [shards(): jnp.einsum('zra,zrf->af', low_all[:, :, t * rank:(t + 1) * rank], stacked...]
    pallas_call x1, Pallas kernels: 4.34 us -> 1.2 us  [down_terms(): pl.pallas_call(down_kernel, in_specs=[pl.BlockSpec(memory_space=pltpu.VME...]
    pallas_call x2 -> x4, Pallas kernels: 7.02 us -> 9.48 us  [the longest x1 4.97 us: pack(): pl.pallas_call(pack_kernel, in_specs=[pl.BlockSpec(memory_space=pltpu.SME...]
    unnamed x3 -> x8, local copies, waits for them, and re-layouts: 1.69 us -> 3.79 us
    ppermute x6 -> x7, waiting for transfers between devices: 11.2 us -> 13.3 us  [the longest x6 11.2 us: sum_windows(): lax.ppermute(x.astype(first), 'dp', [(i, i ^ step) for i in range(n)])]
  transfers between devices with their start and end apart: 13 -> 12, of which waited for: 10 -> 8; matrix products, arithmetic and copies ran while one was open for 5% -> 2% of each run, Pallas kernels for 11% -> 2%
where the time goes in v4:
time: 170 us; the launch traced here: 168 us
  blocking collectives  63.5 us (37%)
  starting transfers between devices  38 us (22%)
  waiting for transfers between devices  31.5 us (19%)
  Pallas kernels  26.8 us (16%)
  local copies, waits for them, and re-layouts  5.76 us (3%)
    all_to_all x1, blocking collectives, swap(): return lax.all_to_all(x, axis, split_axis=0, concat_axis=0, tiled=True)  63.5 us
    all_to_all x3, starting transfers between devices, swap(): return lax.all_to_all(x, axis, split_axis=0, concat_axis=0, tiled=True)  19.6 us
    pallas_call x1, Pallas kernels, attention(): pl.pallas_call(functools.partial(attention_kernel, slots=slots), in_specs...  16.1 us
    all_to_all x3, waiting for transfers between devices, swap(): return lax.all_to_all(x, axis, split_axis=0, concat_axis=0, tiled=True)  12.8 us
    ppermute x6, waiting for transfers between devices, sum_windows(): lax.ppermute(x.astype(first), 'dp', [(i, i ^ step) for i in range(n)])  11.2 us
    ppermute x6, starting transfers between devices, sum_windows(): lax.ppermute(x.astype(first), 'dp', [(i, i ^ step) for i in range(n)])  9.74 us
    ppermute x2, starting transfers between devices, sum_windows(): lax.ppermute(x, 'dp', [(i, (i + (2 if i % 4 >= 2 else -2)) % n) for i in...  8.44 us
    ppermute x2, waiting for transfers between devices, sum_windows(): lax.ppermute(x, 'dp', [(i, (i + (2 if i % 4 >= 2 else -2)) % n) for i in...  5.38 us
  transfers between devices with their start and end apart: 12, of which 8 were waited for; matrix products, arithmetic and copies ran while one was open for 2% of the time, Pallas kernels for 2%

profile of v4, /device:TPU:2, one launch (start us, length us, event | category | flops | bytes accessed | tf_op | source)
XLA Modules:
  0.0 167.9 jit_solution(6215661666940916410)
XLA Ops:
  0.6 5.0 %pack.1 = bf16[32,592,128]{2,1,0:T(8,128)(2,1)} custom-call(s32[2,8]{1,0:T(2,128)} %bitcast.27, s32[1,2]{1,0:T(1,128)} %counts_ref.1, bf16[128,4096]{1,0:T(8,128)(2,1)} %bitcast.18, bf16[128,4096]{1,0:T(8,128)(2,1)} %bitcast.19, bf16[128,4096]{1,0:T(8,128)(2,1)} %bitcast.20, bf16[128,4096]{1,0:T(8,128)(2,1)} %bitcast.21, bf16[128,4096]{1,0:T(8,128)(2,1)} %bitcast.15, ...), custom_call_target="tpu_custom_call" | custom-call | bytes 8388608 | tf_op jit(solution)/shard_map/pack/pallas_call | solution.py:98
  5.6 63.5 %all_to_all.20 = bf16[32,592,128]{2,1,0:T(8,128)(2,1)} all-to-all(bf16[32,592,128]{2,1,0:T(8,128)(2,1)} %pack.1), channel_id=1, replica_groups=mesh['dp'=8,'zone'=32] {'zone'}, dimensions={0} | all-to-all | bytes 9699328 | tf_op jit(solution)/shard_map/all_to_all | solution.py:472
  69.1 16.1 %attention.1 = (bf16[32,256,128]{2,1,0:T(8,128)(2,1)}, bf16[64,64,128]{2,1,0:T(8,128)(2,1)}) custom-call(bf16[32,37,16,128]{3,2,1,0:T(8,128)(2,1)} %bitcast.17), custom_call_target="tpu_custom_call" | custom-call | flops 6039797760 | bytes 7995392 | tf_op jit(solution)/shard_map/attention/pallas_call | solution.py:361
  85.2 5.8 %all-to-all-start.1 = ((bf16[32,256,128]{2,1,0:T(8,128)(2,1)}), bf16[32,256,128]{2,1,0:T(8,128)(2,1)S(1)}, u32[]{:S(2)}, u32[]{:S(2)}) async-start(bf16[32,256,128]{2,1,0:T(8,128)(2,1)} %get-tuple-element.16.grads_ref), calls=%async_computation.1 | async-start | bytes 4194304 | tf_op jit(solution)/shard_map/all_to_all | solution.py:472
  91.1 2.0 %slice.4.own_ref = bf16[32,64,128]{2,1,0:T(8,128)(2,1)} slice(bf16[32,592,128]{2,1,0:T(8,128)(2,1)} %all_to_all.20), slice={[0:32], [528:592], [0:128]} | slice | bytes 1048576 | tf_op jit(solution)/shard_map/slice | solution.py:527
  93.2 2.1 %collective-permute-done.other_ref = bf16[32,64,128]{2,1,0:T(8,128)(2,1)} collective-permute-done((bf16[32,64,128]{2,1,0:T(8,128)(2,1)}, bf16[32,64,128]{2,1,0:T(8,128)(2,1)}, u32[]{:S(2)}, u32[]{:S(2)}) %collective-permute-start) | collective-permute-done | bytes 524320 | tf_op jit(solution)/shard_map/ppermute | solution.py:528
  95.3 1.6 copy-done
  96.9 1.7 %up_terms.1 = f32[128,128]{1,0:T(8,128)S(1)} custom-call(s32[1]{0:T(128)} %bitcast.9.parity_ref, bf16[32,64,128]{2,1,0:T(8,128)(2,1)} %slice.4.own_ref, bf16[32,64,128]{2,1,0:T(8,128)(2,1)} %collective-permute-done.other_ref, bf16[32,256,128]{2,1,0:T(8,128)(2,1)S(1)} %copy-done), custom_call_target="tpu_custom_call" | custom-call | flops 268435456 | bytes 3145728 | tf_op jit(solution)/shard_map/up_terms/pallas_call | solution.py:136
  98.6 2.5 %collective-permute-start.1 = (f32[128,128]{1,0:T(8,128)S(1)}, f32[128,128]{1,0:T(8,128)S(1)}, u32[]{:S(2)}, u32[]{:S(2)}) collective-permute-start(f32[128,128]{1,0:T(8,128)S(1)} %up_terms.1), channel_id=1, source_target_pairs={{0,32},{32,0},{64,96},{96,64},{128,160},{160,128},{192,224},{224,1... | collective-permute-start | bytes 196616 | tf_op jit(solution)/shard_map/ppermute | solution.py:486
  101.1 2.8 %collective-permute-start.2 = (f32[128,128]{1,0:T(8,128)S(1)}, f32[128,128]{1,0:T(8,128)S(1)}, u32[]{:S(2)}, u32[]{:S(2)}) collective-permute-start(f32[128,128]{1,0:T(8,128)S(1)} %up_terms.1), channel_id=1, source_target_pairs={{0,64},{32,96},{64,0},{96,32},{128,192},{160,224},{192,128},{224,1... | collective-permute-start | bytes 196616 | tf_op jit(solution)/shard_map/ppermute | solution.py:486
  103.9 4.8 %collective-permute-done.2 = f32[128,128]{1,0:T(8,128)S(1)} collective-permute-done((f32[128,128]{1,0:T(8,128)S(1)}, f32[128,128]{1,0:T(8,128)S(1)}, u32[]{:S(2)}, u32[]{:S(2)}) %collective-permute-start.2) | collective-permute-done | bytes 65568 | tf_op jit(solution)/shard_map/ppermute | solution.py:486
  108.7 1.4 collective-permute-done.3
  110.1 5.4 %collective-permute-start.4 = (f32[128,128]{1,0:T(8,128)S(1)}, f32[128,128]{1,0:T(8,128)S(1)}, u32[]{:S(2)}, u32[]{:S(2)}) collective-permute-start(f32[128,128]{1,0:T(8,128)S(1)} %add_add_fusion.1), channel_id=1, source_target_pairs={{0,192},{32,224},{64,128},{96,160},{128,64},{160,96},{192,0},{224,... | collective-permute-start | bytes 196616 | tf_op jit(solution)/shard_map/ppermute | solution.py:490
  115.4 2.5 %collective-permute-done.4 = f32[128,128]{1,0:T(8,128)S(1)} collective-permute-done((f32[128,128]{1,0:T(8,128)S(1)}, f32[128,128]{1,0:T(8,128)S(1)}, u32[]{:S(2)}, u32[]{:S(2)}) %collective-permute-start.4) | collective-permute-done | bytes 65568 | tf_op jit(solution)/shard_map/ppermute | solution.py:490
  118.0 1.2 copy-done.3
  119.2 1.2 down_terms.1
  120.4 1.0 copy-done.2
  121.4 7.4 %all-to-all-start.2 = ((bf16[32,128,128]{2,1,0:T(8,128)(2,1)}), bf16[32,128,128]{2,1,0:T(8,128)(2,1)S(1)}, u32[]{:S(2)}, u32[]{:S(2)}) async-start(bf16[32,128,128]{2,1,0:T(8,128)(2,1)} %copy-done.2), calls=%async_computation.2 | async-start | bytes 2097152 | tf_op jit(solution)/shard_map/all_to_all | solution.py:472
  128.8 1.6 unpack.2
  130.4 12.8 %all-to-all-done.2 = bf16[32,128,128]{2,1,0:T(8,128)(2,1)S(1)} async-done(((bf16[32,128,128]{2,1,0:T(8,128)(2,1)}), bf16[32,128,128]{2,1,0:T(8,128)(2,1)S(1)}, u32[]{:S(2)}, u32[]{:S(2)}) %all-to-all-start.2) | async-done | bytes 1048608 | tf_op jit(solution)/shard_map/all_to_all | solution.py:472
  143.2 6.4 %all-to-all-start.3 = ((bf16[32,128,128]{2,1,0:T(8,128)(2,1)}), bf16[32,128,128]{2,1,0:T(8,128)(2,1)S(1)}, u32[]{:S(2)}, u32[]{:S(2)}) async-start(bf16[32,128,128]{2,1,0:T(8,128)(2,1)} %bitcast.23), calls=%async_computation.3 | async-start | bytes 2097152 | tf_op jit(solution)/shard_map/all_to_all | solution.py:472
  149.7 0.2 convert_reduce_fusion
  149.8 1.0 collective-permute-start.5
  150.8 2.8 %collective-permute-start.6 = (bf16[128,128]{1,0:T(8,128)(2,1)S(1)}, bf16[128,128]{1,0:T(8,128)(2,1)S(1)}, u32[]{:S(2)}, u32[]{:S(2)}) collective-permute-start(bf16[128,128]{1,0:T(8,128)(2,1)S(1)} %reduce-precision_convert_fusion), channel_id=1, source_target_pairs={{0,64},{32,96},{64,0},{96,32},{128,192},{160,224},{192,128},{224,1... | collective-permute-start | bytes 98312 | tf_op jit(solution)/shard_map/ppermute | solution.py:486
  153.6 0.7 collective-permute-start.7
  154.3 1.4 collective-permute-done.6
  155.7 3.6 %collective-permute-done.7 = bf16[128,128]{1,0:T(8,128)(2,1)S(1)} collective-permute-done((bf16[128,128]{1,0:T(8,128)(2,1)S(1)}, bf16[128,128]{1,0:T(8,128)(2,1)S(1)}, u32[]{:S(2)}, u32[]{:S(2)}) %collective-permute-start.7) | collective-permute-done | bytes 32800 | tf_op jit(solution)/shard_map/ppermute | solution.py:486
  159.3 3.1 %collective-permute-start.8 = (f32[128,128]{1,0:T(8,128)S(1)}, f32[128,128]{1,0:T(8,128)S(1)}, u32[]{:S(2)}, u32[]{:S(2)}) collective-permute-start(f32[128,128]{1,0:T(8,128)S(1)} %add_add_fusion), channel_id=1, source_target_pairs={{0,192},{32,224},{64,128},{96,160},{128,64},{160,96},{192,0},{224,... | collective-permute-start | bytes 196616 | tf_op jit(solution)/shard_map/ppermute | solution.py:490
  162.4 0.6 broadcast_multiply_fusion
  163.1 2.9 %collective-permute-done.8 = f32[128,128]{1,0:T(8,128)S(1)} collective-permute-done((f32[128,128]{1,0:T(8,128)S(1)}, f32[128,128]{1,0:T(8,128)S(1)}, u32[]{:S(2)}, u32[]{:S(2)}) %collective-permute-start.8) | collective-permute-done | bytes 65568 | tf_op jit(solution)/shard_map/ppermute | solution.py:490
  165.9 0.6 add_multiply_fusion
  166.6 1.2 unpack.3
  (15 shorter events, 0.2 us)
Async XLA Ops:
  85.2 32.7 %all-to-all-start.1 = ((bf16[32,256,128]{2,1,0:T(8,128)(2,1)}), bf16[32,256,128]{2,1,0:T(8,128)(2,1)S(1)}, u32[]{:S(2)}, u32[]{:S(2)}) async-start(bf16[32,256,128]{2,1,0:T(8,128)(2,1)} %get-tuple-element.16.grads_ref), calls=%async_computation.1 | async-start | bytes 4194304 | tf_op jit(solution)/shard_map/all_to_all | solution.py:472
  91.1 26.9 %copy-start.1 = (bf16[1,128,4096]{2,1,0:T(8,128)(2,1)S(1)}, bf16[1,128,4096]{2,1,0:T(8,128)(2,1)}, u32[]{:S(2)}) copy-start(bf16[1,128,4096]{2,1,0:T(8,128)(2,1)} %param.9) | copy-start | bytes 3145732
  93.0 2.3 %collective-permute-start = (bf16[32,64,128]{2,1,0:T(8,128)(2,1)}, bf16[32,64,128]{2,1,0:T(8,128)(2,1)}, u32[]{:S(2)}, u32[]{:S(2)}) collective-permute-start(bf16[32,64,128]{2,1,0:T(8,128)(2,1)} %slice.4.own_ref), channel_id=1, source_target_pairs={{0,1},{1,0},{2,3},{3,2},{4,5},{5,4},{6,7},{7,6},{8,9},{9,8},{10,11... | collective-permute-start | bytes 1572872 | tf_op jit(solution)/shard_map/ppermute | solution.py:528
  95.3 1.6 copy-start
  98.6 5.3 %collective-permute-start.1 = (f32[128,128]{1,0:T(8,128)S(1)}, f32[128,128]{1,0:T(8,128)S(1)}, u32[]{:S(2)}, u32[]{:S(2)}) collective-permute-start(f32[128,128]{1,0:T(8,128)S(1)} %up_terms.1), channel_id=1, source_target_pairs={{0,32},{32,0},{64,96},{96,64},{128,160},{160,128},{192,224},{224,1... | collective-permute-start | bytes 196616 | tf_op jit(solution)/shard_map/ppermute | solution.py:486
  101.1 7.6 %collective-permute-start.2 = (f32[128,128]{1,0:T(8,128)S(1)}, f32[128,128]{1,0:T(8,128)S(1)}, u32[]{:S(2)}, u32[]{:S(2)}) collective-permute-start(f32[128,128]{1,0:T(8,128)S(1)} %up_terms.1), channel_id=1, source_target_pairs={{0,64},{32,96},{64,0},{96,32},{128,192},{160,224},{192,128},{224,1... | collective-permute-start | bytes 196616 | tf_op jit(solution)/shard_map/ppermute | solution.py:486
  103.9 6.2 %collective-permute-start.3 = (f32[128,128]{1,0:T(8,128)S(1)}, f32[128,128]{1,0:T(8,128)S(1)}, u32[]{:S(2)}, u32[]{:S(2)}) collective-permute-start(f32[128,128]{1,0:T(8,128)S(1)} %up_terms.1), channel_id=1, source_target_pairs={{0,96},{32,64},{64,32},{96,0},{128,224},{160,192},{192,160},{224,1... | collective-permute-start | bytes 196616 | tf_op jit(solution)/shard_map/ppermute | solution.py:486
  110.1 7.9 %collective-permute-start.4 = (f32[128,128]{1,0:T(8,128)S(1)}, f32[128,128]{1,0:T(8,128)S(1)}, u32[]{:S(2)}, u32[]{:S(2)}) collective-permute-start(f32[128,128]{1,0:T(8,128)S(1)} %add_add_fusion.1), channel_id=1, source_target_pairs={{0,192},{32,224},{64,128},{96,160},{128,64},{160,96},{192,0},{224,... | collective-permute-start | bytes 196616 | tf_op jit(solution)/shard_map/ppermute | solution.py:490
  118.0 1.2 copy-start.3
  120.4 1.0 copy-start.2
  121.4 21.8 %all-to-all-start.2 = ((bf16[32,128,128]{2,1,0:T(8,128)(2,1)}), bf16[32,128,128]{2,1,0:T(8,128)(2,1)S(1)}, u32[]{:S(2)}, u32[]{:S(2)}) async-start(bf16[32,128,128]{2,1,0:T(8,128)(2,1)} %copy-done.2), calls=%async_computation.2 | async-start | bytes 2097152 | tf_op jit(solution)/shard_map/all_to_all | solution.py:472
  143.2 23.3 %all-to-all-start.3 = ((bf16[32,128,128]{2,1,0:T(8,128)(2,1)}), bf16[32,128,128]{2,1,0:T(8,128)(2,1)S(1)}, u32[]{:S(2)}, u32[]{:S(2)}) async-start(bf16[32,128,128]{2,1,0:T(8,128)(2,1)} %bitcast.23), calls=%async_computation.3 | async-start | bytes 2097152 | tf_op jit(solution)/shard_map/all_to_all | solution.py:472
  149.8 4.5 %collective-permute-start.5 = (bf16[128,128]{1,0:T(8,128)(2,1)S(1)}, bf16[128,128]{1,0:T(8,128)(2,1)S(1)}, u32[]{:S(2)}, u32[]{:S(2)}) collective-permute-start(bf16[128,128]{1,0:T(8,128)(2,1)S(1)} %reduce-precision_convert_fusion), channel_id=1, source_target_pairs={{0,32},{32,0},{64,96},{96,64},{128,160},{160,128},{192,224},{224,1... | collective-permute-start | bytes 98312 | tf_op jit(solution)/shard_map/ppermute | solution.py:486
  150.8 4.9 %collective-permute-start.6 = (bf16[128,128]{1,0:T(8,128)(2,1)S(1)}, bf16[128,128]{1,0:T(8,128)(2,1)S(1)}, u32[]{:S(2)}, u32[]{:S(2)}) collective-permute-start(bf16[128,128]{1,0:T(8,128)(2,1)S(1)} %reduce-precision_convert_fusion), channel_id=1, source_target_pairs={{0,64},{32,96},{64,0},{96,32},{128,192},{160,224},{192,128},{224,1... | collective-permute-start | bytes 98312 | tf_op jit(solution)/shard_map/ppermute | solution.py:486
  153.6 5.7 %collective-permute-start.7 = (bf16[128,128]{1,0:T(8,128)(2,1)S(1)}, bf16[128,128]{1,0:T(8,128)(2,1)S(1)}, u32[]{:S(2)}, u32[]{:S(2)}) collective-permute-start(bf16[128,128]{1,0:T(8,128)(2,1)S(1)} %reduce-precision_convert_fusion), channel_id=1, source_target_pairs={{0,96},{32,64},{64,32},{96,0},{128,224},{160,192},{192,160},{224,1... | collective-permute-start | bytes 98312 | tf_op jit(solution)/shard_map/ppermute | solution.py:486
  159.3 6.6 %collective-permute-start.8 = (f32[128,128]{1,0:T(8,128)S(1)}, f32[128,128]{1,0:T(8,128)S(1)}, u32[]{:S(2)}, u32[]{:S(2)}) collective-permute-start(f32[128,128]{1,0:T(8,128)S(1)} %add_add_fusion), channel_id=1, source_target_pairs={{0,192},{32,224},{64,128},{96,160},{128,64},{160,96},{192,0},{224,... | collective-permute-start | bytes 196616 | tf_op jit(solution)/shard_map/ppermute | solution.py:490

commit v5 on v4

--- a/solution.py
+++ b/solution.py
@@ -313,17 +313,17 @@
     products(0, slots, s_bufs[0], g_bufs[0])
     products(1, slots, s_bufs[1], g_bufs[1])
     softmax(0, slots, s_bufs[0], g_bufs[0], w_bufs[0], d_bufs[0])
-    first, last = 1, pairs // 2 + 1
+    first, last = 0, pairs // 4
     for n in range(slots, least, -1):
 
         def body(i, carry, n=n):
-            step(2 * i, 0, n)
-            step(2 * i + 1, 1, n)
+            for j in range(4):
+                step(4 * i + 2 + j, j % 2, n)
             return carry
 
         until = last
         if n > least + 1:
-            until = jnp.minimum(1 + ((above[n - 2] + 3) >> 2), last)
+            until = (above[n - 2] + 7) >> 3
         lax.fori_loop(first, until, body, 0)
         first = until
 

time: 170 us -> 169 us (level)
  no operation moved by 1% of the time
where the time goes in v5:
time: 169 us; the launch traced here: 168 us
  blocking collectives  63.5 us (38%)
  starting transfers between devices  38.4 us (23%)
  waiting for transfers between devices  30.3 us (18%)
  Pallas kernels  27.2 us (16%)
  local copies, waits for them, and re-layouts  5.76 us (3%)
    all_to_all x1, blocking collectives, swap(): return lax.all_to_all(x, axis, split_axis=0, concat_axis=0, tiled=True)  63.5 us
    all_to_all x3, starting transfers between devices, swap(): return lax.all_to_all(x, axis, split_axis=0, concat_axis=0, tiled=True)  19.7 us
    pallas_call x1, Pallas kernels, attention(): pl.pallas_call(functools.partial(attention_kernel, slots=slots), in_specs...  16.5 us
    all_to_all x3, waiting for transfers between devices, swap(): return lax.all_to_all(x, axis, split_axis=0, concat_axis=0, tiled=True)  12.8 us
    ppermute x6, waiting for transfers between devices, sum_windows(): lax.ppermute(x.astype(first), 'dp', [(i, i ^ step) for i in range(n)])  10.3 us
    ppermute x6, starting transfers between devices, sum_windows(): lax.ppermute(x.astype(first), 'dp', [(i, i ^ step) for i in range(n)])  9.46 us
    ppermute x2, starting transfers between devices, sum_windows(): lax.ppermute(x, 'dp', [(i, (i + (2 if i % 4 >= 2 else -2)) % n) for i in...  9.06 us
    ppermute x2, waiting for transfers between devices, sum_windows(): lax.ppermute(x, 'dp', [(i, (i + (2 if i % 4 >= 2 else -2)) % n) for i in...  5.02 us
  transfers between devices with their start and end apart: 12, of which 8 were waited for; matrix products, arithmetic and copies ran while one was open for 2% of the time, Pallas kernels for 2%

profile of v5, /device:TPU:2, one launch (start us, length us, event | category | flops | bytes accessed | tf_op | source)
XLA Modules:
  0.0 167.5 jit_solution(1270848833339536462)
XLA Ops:
  0.6 5.0 %pack.1 = bf16[32,592,128]{2,1,0:T(8,128)(2,1)} custom-call(s32[2,8]{1,0:T(2,128)} %bitcast.27, s32[1,2]{1,0:T(1,128)} %counts_ref.1, bf16[128,4096]{1,0:T(8,128)(2,1)} %bitcast.18, bf16[128,4096]{1,0:T(8,128)(2,1)} %bitcast.19, bf16[128,4096]{1,0:T(8,128)(2,1)} %bitcast.20, bf16[128,4096]{1,0:T(8,128)(2,1)} %bitcast.21, bf16[128,4096]{1,0:T(8,128)(2,1)} %bitcast.15, ...), custom_call_target="tpu_custom_call" | custom-call | bytes 8388608 | tf_op jit(solution)/shard_map/pack/pallas_call | solution.py:98
  5.6 63.5 %all_to_all.20 = bf16[32,592,128]{2,1,0:T(8,128)(2,1)} all-to-all(bf16[32,592,128]{2,1,0:T(8,128)(2,1)} %pack.1), channel_id=1, replica_groups=mesh['dp'=8,'zone'=32] {'zone'}, dimensions={0} | all-to-all | bytes 9699328 | tf_op jit(solution)/shard_map/all_to_all | solution.py:472
  69.1 16.5 %attention.1 = (bf16[32,256,128]{2,1,0:T(8,128)(2,1)}, bf16[64,64,128]{2,1,0:T(8,128)(2,1)}) custom-call(bf16[32,37,16,128]{3,2,1,0:T(8,128)(2,1)} %bitcast.17), custom_call_target="tpu_custom_call" | custom-call | flops 6039797760 | bytes 7995392 | tf_op jit(solution)/shard_map/attention/pallas_call | solution.py:361
  85.6 5.8 %all-to-all-start.1 = ((bf16[32,256,128]{2,1,0:T(8,128)(2,1)}), bf16[32,256,128]{2,1,0:T(8,128)(2,1)S(1)}, u32[]{:S(2)}, u32[]{:S(2)}) async-start(bf16[32,256,128]{2,1,0:T(8,128)(2,1)} %get-tuple-element.16.grads_ref), calls=%async_computation.1 | async-start | bytes 4194304 | tf_op jit(solution)/shard_map/all_to_all | solution.py:472
  91.5 2.0 %slice.4.own_ref = bf16[32,64,128]{2,1,0:T(8,128)(2,1)} slice(bf16[32,592,128]{2,1,0:T(8,128)(2,1)} %all_to_all.20), slice={[0:32], [528:592], [0:128]} | slice | bytes 1048576 | tf_op jit(solution)/shard_map/slice | solution.py:527
  93.6 2.1 %collective-permute-done.other_ref = bf16[32,64,128]{2,1,0:T(8,128)(2,1)} collective-permute-done((bf16[32,64,128]{2,1,0:T(8,128)(2,1)}, bf16[32,64,128]{2,1,0:T(8,128)(2,1)}, u32[]{:S(2)}, u32[]{:S(2)}) %collective-permute-start) | collective-permute-done | bytes 524320 | tf_op jit(solution)/shard_map/ppermute | solution.py:528
  95.7 1.6 copy-done
  97.3 1.7 %up_terms.1 = f32[128,128]{1,0:T(8,128)S(1)} custom-call(s32[1]{0:T(128)} %bitcast.9.parity_ref, bf16[32,64,128]{2,1,0:T(8,128)(2,1)} %slice.4.own_ref, bf16[32,64,128]{2,1,0:T(8,128)(2,1)} %collective-permute-done.other_ref, bf16[32,256,128]{2,1,0:T(8,128)(2,1)S(1)} %copy-done), custom_call_target="tpu_custom_call" | custom-call | flops 268435456 | bytes 3145728 | tf_op jit(solution)/shard_map/up_terms/pallas_call | solution.py:136
  99.0 2.0 %collective-permute-start.1 = (f32[128,128]{1,0:T(8,128)S(1)}, f32[128,128]{1,0:T(8,128)S(1)}, u32[]{:S(2)}, u32[]{:S(2)}) collective-permute-start(f32[128,128]{1,0:T(8,128)S(1)} %up_terms.1), channel_id=1, source_target_pairs={{0,32},{32,0},{64,96},{96,64},{128,160},{160,128},{192,224},{224,1... | collective-permute-start | bytes 196616 | tf_op jit(solution)/shard_map/ppermute | solution.py:486
  101.0 2.5 %collective-permute-start.2 = (f32[128,128]{1,0:T(8,128)S(1)}, f32[128,128]{1,0:T(8,128)S(1)}, u32[]{:S(2)}, u32[]{:S(2)}) collective-permute-start(f32[128,128]{1,0:T(8,128)S(1)} %up_terms.1), channel_id=1, source_target_pairs={{0,64},{32,96},{64,0},{96,32},{128,192},{160,224},{192,128},{224,1... | collective-permute-start | bytes 196616 | tf_op jit(solution)/shard_map/ppermute | solution.py:486
  103.6 0.4 collective-permute-start.3
  104.0 4.6 %collective-permute-done.2 = f32[128,128]{1,0:T(8,128)S(1)} collective-permute-done((f32[128,128]{1,0:T(8,128)S(1)}, f32[128,128]{1,0:T(8,128)S(1)}, u32[]{:S(2)}, u32[]{:S(2)}) %collective-permute-start.2) | collective-permute-done | bytes 65568 | tf_op jit(solution)/shard_map/ppermute | solution.py:486
  108.6 1.1 collective-permute-done.3
  109.7 5.9 %collective-permute-start.4 = (f32[128,128]{1,0:T(8,128)S(1)}, f32[128,128]{1,0:T(8,128)S(1)}, u32[]{:S(2)}, u32[]{:S(2)}) collective-permute-start(f32[128,128]{1,0:T(8,128)S(1)} %add_add_fusion.1), channel_id=1, source_target_pairs={{0,192},{32,224},{64,128},{96,160},{128,64},{160,96},{192,0},{224,... | collective-permute-start | bytes 196616 | tf_op jit(solution)/shard_map/ppermute | solution.py:490
  115.6 2.4 %collective-permute-done.4 = f32[128,128]{1,0:T(8,128)S(1)} collective-permute-done((f32[128,128]{1,0:T(8,128)S(1)}, f32[128,128]{1,0:T(8,128)S(1)}, u32[]{:S(2)}, u32[]{:S(2)}) %collective-permute-start.4) | collective-permute-done | bytes 65568 | tf_op jit(solution)/shard_map/ppermute | solution.py:490
  118.0 1.2 copy-done.3
  119.3 1.2 down_terms.1
  120.5 1.0 copy-done.2
  121.4 7.5 %all-to-all-start.2 = ((bf16[32,128,128]{2,1,0:T(8,128)(2,1)}), bf16[32,128,128]{2,1,0:T(8,128)(2,1)S(1)}, u32[]{:S(2)}, u32[]{:S(2)}) async-start(bf16[32,128,128]{2,1,0:T(8,128)(2,1)} %copy-done.2), calls=%async_computation.2 | async-start | bytes 2097152 | tf_op jit(solution)/shard_map/all_to_all | solution.py:472
  128.9 1.6 unpack.2
  130.5 12.8 %all-to-all-done.2 = bf16[32,128,128]{2,1,0:T(8,128)(2,1)S(1)} async-done(((bf16[32,128,128]{2,1,0:T(8,128)(2,1)}), bf16[32,128,128]{2,1,0:T(8,128)(2,1)S(1)}, u32[]{:S(2)}, u32[]{:S(2)}) %all-to-all-start.2) | async-done | bytes 1048608 | tf_op jit(solution)/shard_map/all_to_all | solution.py:472
  143.3 6.4 %all-to-all-start.3 = ((bf16[32,128,128]{2,1,0:T(8,128)(2,1)}), bf16[32,128,128]{2,1,0:T(8,128)(2,1)S(1)}, u32[]{:S(2)}, u32[]{:S(2)}) async-start(bf16[32,128,128]{2,1,0:T(8,128)(2,1)} %bitcast.23), calls=%async_computation.3 | async-start | bytes 2097152 | tf_op jit(solution)/shard_map/all_to_all | solution.py:472
  149.9 1.6 collective-permute-start.5
  151.6 1.8 %collective-permute-start.6 = (bf16[128,128]{1,0:T(8,128)(2,1)S(1)}, bf16[128,128]{1,0:T(8,128)(2,1)S(1)}, u32[]{:S(2)}, u32[]{:S(2)}) collective-permute-start(bf16[128,128]{1,0:T(8,128)(2,1)S(1)} %reduce-precision_convert_fusion), channel_id=1, source_target_pairs={{0,64},{32,96},{64,0},{96,32},{128,192},{160,224},{192,128},{224,1... | collective-permute-start | bytes 98312 | tf_op jit(solution)/shard_map/ppermute | solution.py:486
  153.3 1.1 collective-permute-start.7
  154.4 2.6 %collective-permute-done.6 = bf16[128,128]{1,0:T(8,128)(2,1)S(1)} collective-permute-done((bf16[128,128]{1,0:T(8,128)(2,1)S(1)}, bf16[128,128]{1,0:T(8,128)(2,1)S(1)}, u32[]{:S(2)}, u32[]{:S(2)}) %collective-permute-start.6) | collective-permute-done | bytes 32800 | tf_op jit(solution)/shard_map/ppermute | solution.py:486
  157.0 2.0 %collective-permute-done.7 = bf16[128,128]{1,0:T(8,128)(2,1)S(1)} collective-permute-done((bf16[128,128]{1,0:T(8,128)(2,1)S(1)}, bf16[128,128]{1,0:T(8,128)(2,1)S(1)}, u32[]{:S(2)}, u32[]{:S(2)}) %collective-permute-start.7) | collective-permute-done | bytes 32800 | tf_op jit(solution)/shard_map/ppermute | solution.py:486
  159.1 3.2 %collective-permute-start.8 = (f32[128,128]{1,0:T(8,128)S(1)}, f32[128,128]{1,0:T(8,128)S(1)}, u32[]{:S(2)}, u32[]{:S(2)}) collective-permute-start(f32[128,128]{1,0:T(8,128)S(1)} %add_add_fusion), channel_id=1, source_target_pairs={{0,192},{32,224},{64,128},{96,160},{128,64},{160,96},{192,0},{224,... | collective-permute-start | bytes 196616 | tf_op jit(solution)/shard_map/ppermute | solution.py:490
  162.2 0.6 broadcast_multiply_fusion
  162.9 2.7 %collective-permute-done.8 = f32[128,128]{1,0:T(8,128)S(1)} collective-permute-done((f32[128,128]{1,0:T(8,128)S(1)}, f32[128,128]{1,0:T(8,128)S(1)}, u32[]{:S(2)}, u32[]{:S(2)}) %collective-permute-start.8) | collective-permute-done | bytes 65568 | tf_op jit(solution)/shard_map/ppermute | solution.py:490
  165.5 0.6 add_multiply_fusion
  166.2 1.2 unpack.3
  (15 shorter events, 0.4 us)
Async XLA Ops:
  85.6 32.4 %all-to-all-start.1 = ((bf16[32,256,128]{2,1,0:T(8,128)(2,1)}), bf16[32,256,128]{2,1,0:T(8,128)(2,1)S(1)}, u32[]{:S(2)}, u32[]{:S(2)}) async-start(bf16[32,256,128]{2,1,0:T(8,128)(2,1)} %get-tuple-element.16.grads_ref), calls=%async_computation.1 | async-start | bytes 4194304 | tf_op jit(solution)/shard_map/all_to_all | solution.py:472
  91.5 26.6 %copy-start.1 = (bf16[1,128,4096]{2,1,0:T(8,128)(2,1)S(1)}, bf16[1,128,4096]{2,1,0:T(8,128)(2,1)}, u32[]{:S(2)}) copy-start(bf16[1,128,4096]{2,1,0:T(8,128)(2,1)} %param.9) | copy-start | bytes 3145732
  93.4 2.3 %collective-permute-start = (bf16[32,64,128]{2,1,0:T(8,128)(2,1)}, bf16[32,64,128]{2,1,0:T(8,128)(2,1)}, u32[]{:S(2)}, u32[]{:S(2)}) collective-permute-start(bf16[32,64,128]{2,1,0:T(8,128)(2,1)} %slice.4.own_ref), channel_id=1, source_target_pairs={{0,1},{1,0},{2,3},{3,2},{4,5},{5,4},{6,7},{7,6},{8,9},{9,8},{10,11... | collective-permute-start | bytes 1572872 | tf_op jit(solution)/shard_map/ppermute | solution.py:528
  95.7 1.6 copy-start
  99.0 5.0 %collective-permute-start.1 = (f32[128,128]{1,0:T(8,128)S(1)}, f32[128,128]{1,0:T(8,128)S(1)}, u32[]{:S(2)}, u32[]{:S(2)}) collective-permute-start(f32[128,128]{1,0:T(8,128)S(1)} %up_terms.1), channel_id=1, source_target_pairs={{0,32},{32,0},{64,96},{96,64},{128,160},{160,128},{192,224},{224,1... | collective-permute-start | bytes 196616 | tf_op jit(solution)/shard_map/ppermute | solution.py:486
  101.0 7.5 %collective-permute-start.2 = (f32[128,128]{1,0:T(8,128)S(1)}, f32[128,128]{1,0:T(8,128)S(1)}, u32[]{:S(2)}, u32[]{:S(2)}) collective-permute-start(f32[128,128]{1,0:T(8,128)S(1)} %up_terms.1), channel_id=1, source_target_pairs={{0,64},{32,96},{64,0},{96,32},{128,192},{160,224},{192,128},{224,1... | collective-permute-start | bytes 196616 | tf_op jit(solution)/shard_map/ppermute | solution.py:486
  103.6 6.2 %collective-permute-start.3 = (f32[128,128]{1,0:T(8,128)S(1)}, f32[128,128]{1,0:T(8,128)S(1)}, u32[]{:S(2)}, u32[]{:S(2)}) collective-permute-start(f32[128,128]{1,0:T(8,128)S(1)} %up_terms.1), channel_id=1, source_target_pairs={{0,96},{32,64},{64,32},{96,0},{128,224},{160,192},{192,160},{224,1... | collective-permute-start | bytes 196616 | tf_op jit(solution)/shard_map/ppermute | solution.py:486
  109.7 8.3 %collective-permute-start.4 = (f32[128,128]{1,0:T(8,128)S(1)}, f32[128,128]{1,0:T(8,128)S(1)}, u32[]{:S(2)}, u32[]{:S(2)}) collective-permute-start(f32[128,128]{1,0:T(8,128)S(1)} %add_add_fusion.1), channel_id=1, source_target_pairs={{0,192},{32,224},{64,128},{96,160},{128,64},{160,96},{192,0},{224,... | collective-permute-start | bytes 196616 | tf_op jit(solution)/shard_map/ppermute | solution.py:490
  118.0 1.2 copy-start.3
  120.5 1.0 copy-start.2
  121.4 21.9 %all-to-all-start.2 = ((bf16[32,128,128]{2,1,0:T(8,128)(2,1)}), bf16[32,128,128]{2,1,0:T(8,128)(2,1)S(1)}, u32[]{:S(2)}, u32[]{:S(2)}) async-start(bf16[32,128,128]{2,1,0:T(8,128)(2,1)} %copy-done.2), calls=%async_computation.2 | async-start | bytes 2097152 | tf_op jit(solution)/shard_map/all_to_all | solution.py:472
  143.3 22.8 %all-to-all-start.3 = ((bf16[32,128,128]{2,1,0:T(8,128)(2,1)}), bf16[32,128,128]{2,1,0:T(8,128)(2,1)S(1)}, u32[]{:S(2)}, u32[]{:S(2)}) async-start(bf16[32,128,128]{2,1,0:T(8,128)(2,1)} %bitcast.23), calls=%async_computation.3 | async-start | bytes 2097152 | tf_op jit(solution)/shard_map/all_to_all | solution.py:472
  149.9 4.5 %collective-permute-start.5 = (bf16[128,128]{1,0:T(8,128)(2,1)S(1)}, bf16[128,128]{1,0:T(8,128)(2,1)S(1)}, u32[]{:S(2)}, u32[]{:S(2)}) collective-permute-start(bf16[128,128]{1,0:T(8,128)(2,1)S(1)} %reduce-precision_convert_fusion), channel_id=1, source_target_pairs={{0,32},{32,0},{64,96},{96,64},{128,160},{160,128},{192,224},{224,1... | collective-permute-start | bytes 98312 | tf_op jit(solution)/shard_map/ppermute | solution.py:486
  151.6 5.4 %collective-permute-start.6 = (bf16[128,128]{1,0:T(8,128)(2,1)S(1)}, bf16[128,128]{1,0:T(8,128)(2,1)S(1)}, u32[]{:S(2)}, u32[]{:S(2)}) collective-permute-start(bf16[128,128]{1,0:T(8,128)(2,1)S(1)} %reduce-precision_convert_fusion), channel_id=1, source_target_pairs={{0,64},{32,96},{64,0},{96,32},{128,192},{160,224},{192,128},{224,1... | collective-permute-start | bytes 98312 | tf_op jit(solution)/shard_map/ppermute | solution.py:486
  153.3 5.7 %collective-permute-start.7 = (bf16[128,128]{1,0:T(8,128)(2,1)S(1)}, bf16[128,128]{1,0:T(8,128)(2,1)S(1)}, u32[]{:S(2)}, u32[]{:S(2)}) collective-permute-start(bf16[128,128]{1,0:T(8,128)(2,1)S(1)} %reduce-precision_convert_fusion), channel_id=1, source_target_pairs={{0,96},{32,64},{64,32},{96,0},{128,224},{160,192},{192,160},{224,1... | collective-permute-start | bytes 98312 | tf_op jit(solution)/shard_map/ppermute | solution.py:486
  159.1 6.5 %collective-permute-start.8 = (f32[128,128]{1,0:T(8,128)S(1)}, f32[128,128]{1,0:T(8,128)S(1)}, u32[]{:S(2)}, u32[]{:S(2)}) collective-permute-start(f32[128,128]{1,0:T(8,128)S(1)} %add_add_fusion), channel_id=1, source_target_pairs={{0,192},{32,224},{64,128},{96,160},{128,64},{160,96},{192,0},{224,... | collective-permute-start | bytes 196616 | tf_op jit(solution)/shard_map/ppermute | solution.py:490
